TPU v7x, 512 devices: a whole 4x4x16 slice. The times are simulated.
512 devices in a mesh: dp: 4 (over y_hi, core), ctx: 128 (over y_lo, z, x).
Axes of the slice: x: 4, y: 4 (y_hi: 2, y_lo: 2; y = y_hi * 2 + y_lo), z: 16, core: 2. Of those that a mesh axis runs over, the one named last changes fastest.
Arguments:
- queries: bfloat16 [4, 32768, 768], P('dp', 'ctx'), may hold values from -12 to 12
- key_rows: bfloat16 [4, 32768, 768], P('dp', 'ctx'), may hold values from -6 to 6
- value_rows: bfloat16 [4, 32768, 768], P('dp', 'ctx'), may hold values from -6 to 6
- out_weight: bfloat16 [768, 768], P('ctx'), may hold values from -0.21875 to 0.21875
- cotangent: bfloat16 [4, 32768, 768], P('dp', 'ctx'), may hold values from -24 to 24
Outputs:
- grad_queries: bfloat16 [4, 32768, 768], P('dp', 'ctx')
- grad_keys: bfloat16 [4, 32768, 768], P('dp', 'ctx')
- grad_values: bfloat16 [4, 32768, 768], P('dp', 'ctx')
- grad_weight: float32 [768, 768], P('ctx')
All inputs are finite; a program needn't handle non-finite values.
Results may differ from a plain program's by a relative error of at most 0.025.
Values may be sent and summed in bfloat16 or wider, within the bound.
A program may use at most 64 MiB of HBM per device.

v0:
```python
from functools import partial

import jax
import jax.numpy as jnp
from jax import lax
from jax.sharding import PartitionSpec as P

HS = 96
HR = 4
HC = 4
STRIDE = 1024


def from_behind(value, axis, by):
    size = lax.axis_size(axis)
    pairs = [(i, i + by) for i in range(size) if 0 <= i + by < size]
    return lax.ppermute(value, axis, pairs)


def score_grads(probs, out_heads, value_heads, deltas):
    dprobs = jnp.einsum("qhd,khd->hqk", out_heads, value_heads, preferred_element_type=jnp.float32)
    return (probs * (dprobs - deltas[:, :, None]) * HS ** (-0.5)).astype(jnp.bfloat16)


def softmax_parts(query_heads, key_heads, value_heads, out_heads, allowed):
    scores = jnp.einsum(
        "qhd,khd->hqk", query_heads, key_heads, preferred_element_type=jnp.float32
    ) * HS ** (-0.5)
    scores = jnp.where(allowed[None], scores, -1e30)
    row_max = jnp.max(scores, axis=-1, keepdims=True)
    log_total = row_max + jnp.log(jnp.sum(jnp.exp(scores - row_max), axis=-1, keepdims=True))
    probs = jnp.exp(scores - log_total)
    probs_half = probs.astype(jnp.bfloat16)
    attended = jnp.einsum(
        "hqk,khd->qhd", probs_half, value_heads, preferred_element_type=jnp.float32
    ).astype(jnp.bfloat16)
    deltas = jnp.sum(out_heads.astype(jnp.float32) * attended.astype(jnp.float32), axis=-1).T
    dscores = score_grads(probs, out_heads, value_heads, deltas)
    return (probs_half, log_total, attended, deltas, dscores)


def local_grads(query_heads, key_heads, value_heads, out_heads, allowed):
    probs_half, log_total, attended, deltas, dscores = softmax_parts(
        query_heads, key_heads, value_heads, out_heads, allowed
    )
    grad_query = jnp.einsum("hqk,khd->qhd", dscores, key_heads, preferred_element_type=jnp.float32)
    grad_key = jnp.einsum("hqk,qhd->khd", dscores, query_heads, preferred_element_type=jnp.float32)
    grad_value = jnp.einsum(
        "hqk,qhd->khd", probs_half, out_heads, preferred_element_type=jnp.float32
    )
    return (
        attended,
        grad_query.astype(jnp.bfloat16),
        grad_key.astype(jnp.bfloat16),
        grad_value.astype(jnp.bfloat16),
    )


def body(queries, key_rows, value_rows, out_weight, cotangent):
    tok_rows = queries.shape[1]
    row_width = HR * HS
    ctx_count = lax.axis_size("ctx")
    device = lax.axis_index("ctx")
    groups = STRIDE // tok_rows
    cot_rows = cotangent[0]
    columns = cot_rows
    grad_out = jnp.dot(
        columns,
        lax.all_gather(out_weight, "ctx", axis=0, tiled=True),
        preferred_element_type=jnp.float32,
    ).astype(jnp.bfloat16)
    query_all = queries[0]
    key_all = key_rows[0]
    value_all = value_rows[0]
    moved = (
        lax.all_to_all(query_all[:, row_width:], "ctx", split_axis=0, concat_axis=0, tiled=True),
        lax.all_to_all(key_all[:, row_width:], "ctx", split_axis=0, concat_axis=0, tiled=True),
        lax.all_to_all(value_all[:, row_width:], "ctx", split_axis=0, concat_axis=0, tiled=True),
        lax.all_to_all(grad_out[:, row_width:], "ctx", split_axis=0, concat_axis=0, tiled=True),
    )
    per_class = tok_rows // ctx_count
    blocks_count = ctx_count // groups

    def to_classes(block):
        return block.reshape(blocks_count, groups * per_class, HC, HS).transpose(1, 0, 2, 3)

    def to_tokens(block):
        return block.transpose(1, 0, 2, 3).reshape(tok_rows, HC * HS)

    causal_blocks = jnp.tril(jnp.ones((blocks_count, blocks_count), dtype=bool))
    class_out = jax.vmap(partial(local_grads, allowed=causal_blocks))(
        to_classes(moved[0]), to_classes(moved[1]), to_classes(moved[2]), to_classes(moved[3])
    )
    returned = (
        lax.all_to_all(to_tokens(class_out[0]), "ctx", split_axis=0, concat_axis=0, tiled=True),
        lax.all_to_all(to_tokens(class_out[1]), "ctx", split_axis=0, concat_axis=0, tiled=True),
        lax.all_to_all(to_tokens(class_out[2]), "ctx", split_axis=0, concat_axis=0, tiled=True),
        lax.all_to_all(to_tokens(class_out[3]), "ctx", split_axis=0, concat_axis=0, tiled=True),
    )
    row_query = query_all[:, :row_width]
    row_key = key_all[:, :row_width]
    row_value = value_all[:, :row_width]
    row_out = grad_out[:, :row_width]
    key_pieces = []
    value_pieces = []
    for offset in range(groups - 1, 0, -1):
        moved_key, moved_value = from_behind((row_key, row_value), "ctx", offset)
        key_pieces.append(moved_key)
        value_pieces.append(moved_value)
    key_pieces.append(row_key)
    value_pieces.append(row_value)
    key_heads = jnp.concatenate(key_pieces, 0).reshape(groups * tok_rows, HR, HS)
    value_heads = jnp.concatenate(value_pieces, 0).reshape(groups * tok_rows, HR, HS)
    query_heads = row_query.reshape(tok_rows, HR, HS)
    out_heads = row_out.reshape(tok_rows, HR, HS)
    query_pos = device * tok_rows + jnp.arange(tok_rows, dtype=jnp.int32)
    key_pos = (device - groups + 1) * tok_rows + jnp.arange(groups * tok_rows, dtype=jnp.int32)
    allowed = (key_pos[None, :] // STRIDE == query_pos[:, None] // STRIDE) & (
        key_pos[None, :] <= query_pos[:, None]
    )
    probs_half, log_total, row_att, deltas, dscores = softmax_parts(
        query_heads, key_heads, value_heads, out_heads, allowed
    )
    row_grad_query = jnp.einsum(
        "hqk,khd->qhd", dscores, key_heads, preferred_element_type=jnp.float32
    )
    row_grad_query = row_grad_query.astype(jnp.bfloat16).reshape(tok_rows, row_width)
    key_terms = jnp.einsum("hqk,qhd->khd", dscores, query_heads, preferred_element_type=jnp.float32)
    value_terms = jnp.einsum(
        "hqk,qhd->khd", probs_half, out_heads, preferred_element_type=jnp.float32
    )
    key_terms = key_terms.reshape(groups * tok_rows, row_width)
    value_terms = value_terms.reshape(groups * tok_rows, row_width)
    own_key = key_terms[(groups - 1) * tok_rows :]
    own_value = value_terms[(groups - 1) * tok_rows :]
    for offset in range(1, groups):
        first_row = (groups - 1 - offset) * tok_rows
        back_key, back_value = from_behind(
            (
                key_terms[first_row : first_row + tok_rows],
                value_terms[first_row : first_row + tok_rows],
            ),
            "ctx",
            -offset,
        )
        own_key = own_key + back_key
        own_value = own_value + back_value
    attended_all = jnp.concatenate([row_att.reshape(tok_rows, row_width), returned[0]], axis=1)
    grad_queries = jnp.concatenate([row_grad_query, returned[1]], axis=1)
    grad_keys = jnp.concatenate([own_key.astype(jnp.bfloat16), returned[2]], axis=1)
    grad_values = jnp.concatenate([own_value.astype(jnp.bfloat16), returned[3]], axis=1)
    columns = cot_rows
    weight_shard = lax.psum_scatter(
        lax.dot_general(
            columns, attended_all, (((0,), (0,)), ((), ())), preferred_element_type=jnp.float32
        ),
        "ctx",
        scatter_dimension=0,
        tiled=True,
    )
    grad_weight = lax.psum(weight_shard, "dp")
    return (grad_queries[None], grad_keys[None], grad_values[None], grad_weight)


def solution(mesh):
    in_specs = (
        P("dp", "ctx", None),
        P("dp", "ctx", None),
        P("dp", "ctx", None),
        P("ctx", None),
        P("dp", "ctx", None),
    )
    out_specs = (P("dp", "ctx", None), P("dp", "ctx", None), P("dp", "ctx", None), P("ctx", None))
    return jax.shard_map(body, mesh=mesh, in_specs=in_specs, out_specs=out_specs, check_vma=False)
```

profile of v0, /device:TPU:25, one launch (start us, length us, event | category | flops | bytes accessed | tf_op | source)
XLA Modules:
  0.0 1922.1 jit_solution(9061093726508208150)
XLA Ops:
  7.2 1.1 fusion.44
  9.0 20.1 %all-to-all-start = ((bf16[128,2,384]{2,1,0:T(2,128)(2,1)}), bf16[128,2,384]{2,1,0:T(2,128)(2,1)S(1)}, u32[]{:S(2)}, u32[]{:S(2)}) async-start(bf16[128,2,384]{2,1,0:T(2,128)(2,1)} %all_to_all.56), calls=%async_computation | async-start | bytes 393216 | tf_op jit(solution)/shard_map/all_to_all | solution.py:76
  29.2 1.1 fusion.45
  30.2 3.1 collective-permute-start.2
  33.3 4.3 collective-permute-start.1
  37.7 4.0 collective-permute-start
  42.4 8.7 all-to-all-done
  51.1 5.3 all-to-all-start.1
  57.6 2.9 collective-permute-start.5
  60.5 4.3 collective-permute-start.4
  65.8 1.3 dynamic-slice
  68.1 4.0 collective-permute-start.3
  74.1 12.7 all-to-all-start.3
  86.9 2.9 fusion.1
  89.8 1.1 pad_maximum_fusion.1
  90.9 1.2 copy.67
  92.0 3.1 exponential_reduce_fusion
  96.2 6.8 all-to-all-done.3
  104.4 458.8 %all-gather.3.cloned.1.call-done = bf16[128,6,768]{2,1,0:T(8,128)(2,1)} async-done(((bf16[1,6,768]{2,1,0:T(8,128)(2,1)}), bf16[128,6,768]{2,1,0:T(8,128)(2,1)}) %all-gather.3.cloned.1.call-update) | async-done | bytes 1179664 | tf_op jit(solution)/shard_map/all_gather | solution.py:69
  563.3 2.3 reshape.240
  567.7 7.9 all-to-all-start.2
  575.7 3.6 convolution_bitcast_fusion.1
  579.3 3.6 multiply_reduce_fusion
  582.9 8.8 all-to-all-done.2
  591.7 1.9 reshape.236
  593.5 2.1 fusion.9
  595.8 1.2 all_to_all.73
  596.9 8.3 all-to-all-start.7
  605.2 1.2 fusion.40
  606.4 1.7 copy.93
  609.0 6.9 collective-permute-start.10
  616.0 4.2 multiply_convert_fusion
  621.3 2.1 all_to_all.70
  623.4 13.1 all-to-all-start.6
  636.6 1.7 all_to_all.75
  638.3 3.0 convolution_bitcast_fusion
  641.3 1.4 fusion.5
  643.4 1.2 fusion.7
  644.7 1.2 all_to_all.67
  645.9 6.6 all-to-all-done.6
  652.4 10.5 all-to-all-start.5
  662.9 1.7 convolution_bitcast_fusion.2
  664.6 1.2 fusion.41
  665.8 1.9 copy.81
  667.7 1.9 copy.84
  669.6 1.9 copy.87
  671.5 2.0 copy.90
  673.5 1.9 copy.83
  675.4 6.7 collective-permute-start.7
  682.1 3.1 collective-permute-start.11
  685.2 4.3 collective-permute-start.9
  689.5 1.9 collective-permute-start.8
  691.4 1.2 fusion.6
  692.8 1.2 all_to_all.64
  694.0 5.4 collective-permute-start.6
  699.4 10.8 all-to-all-start.4
  710.9 1.2 copy.88
  712.1 1.2 copy.82
  713.2 1.3 add_convert_fusion
  714.6 1.3 add_convert_fusion.1
  717.9 8.3 all-to-all-done.4
  729.5 1094.9 %all-reduce.3.cloned.1.call-done = f32[768,768]{0,1:T(8,128)} async-done(((f32[768,768]{0,1:T(8,128)}), f32[768,768]{0,1:T(8,128)}) %all-reduce.3.cloned.1.call-update) | async-done | bytes 2359312
  1824.5 1.3 constant_dynamic-slice_fusion
  1825.7 88.7 %psum.7 = f32[6,768]{0,1:T(8,128)S(1)} all-reduce(f32[6,768]{0,1:T(8,128)S(1)} %constant_dynamic-slice_fusion), channel_id=1, replica_groups=mesh['dp'=4,'ctx'=128] {'dp'}, use_global_device_ids=true, to_apply=%region_7.8 | all-reduce | flops 4608 | bytes 36864 | tf_op jit(solution)/shard_map/psum | solution.py:161
  (80 shorter events, 20.5 us)
Async XLA Ops:
  7.2 558.4 %copy-start = (bf16[1,256,768]{2,1,0:T(8,128)(2,1)S(1)}, bf16[1,256,768]{2,1,0:T(8,128)(2,1)}, u32[]{:S(2)}) copy-start(bf16[1,256,768]{2,1,0:T(8,128)(2,1)} %param.9) | copy-start | bytes 1179652
  9.0 42.1 %all-to-all-start = ((bf16[128,2,384]{2,1,0:T(2,128)(2,1)}), bf16[128,2,384]{2,1,0:T(2,128)(2,1)S(1)}, u32[]{:S(2)}, u32[]{:S(2)}) async-start(bf16[128,2,384]{2,1,0:T(2,128)(2,1)} %all_to_all.56), calls=%async_computation | async-start | bytes 393216 | tf_op jit(solution)/shard_map/all_to_all | solution.py:76
  30.2 37.9 %collective-permute-start.2 = (bf16[256,384]{1,0:T(8,128)(2,1)S(1)}, bf16[256,384]{1,0:T(8,128)(2,1)S(1)}, u32[]{:S(2)}, u32[]{:S(2)}) collective-permute-start(bf16[256,384]{1,0:T(8,128)(2,1)S(1)} %get-tuple-element.30), channel_id=1, source_target_pairs={{0,1},{1,2},{2,3},{3,4},{4,5},{5,6},{6,7},{7,8},{8,9},{9,10},{10,1... | collective-permute-start | bytes 589832 | tf_op jit(solution)/shard_map/ppermute | solution.py:17
  33.3 38.8 %collective-permute-start.1 = (bf16[256,384]{1,0:T(8,128)(2,1)S(1)}, bf16[256,384]{1,0:T(8,128)(2,1)S(1)}, u32[]{:S(2)}, u32[]{:S(2)}) collective-permute-start(bf16[256,384]{1,0:T(8,128)(2,1)S(1)} %get-tuple-element.30), channel_id=1, source_target_pairs={{0,2},{1,3},{2,4},{3,5},{4,6},{5,7},{6,8},{7,9},{8,10},{9,11},{10,... | collective-permute-start | bytes 589832 | tf_op jit(solution)/shard_map/ppermute | solution.py:17
  37.7 34.5 %collective-permute-start = (bf16[256,384]{1,0:T(8,128)(2,1)S(1)}, bf16[256,384]{1,0:T(8,128)(2,1)}, u32[]{:S(2)}, u32[]{:S(2)}) collective-permute-start(bf16[256,384]{1,0:T(8,128)(2,1)S(1)} %get-tuple-element.30), channel_id=1, source_target_pairs={{0,3},{1,4},{2,5},{3,6},{4,7},{5,8},{6,9},{7,10},{8,11},{9,12},{10... | collective-permute-start | bytes 589832 | tf_op jit(solution)/shard_map/ppermute | solution.py:17
  51.1 23.0 %all-to-all-start.1 = ((bf16[128,2,384]{2,1,0:T(2,128)(2,1)}), bf16[128,2,384]{2,1,0:T(2,128)(2,1)S(1)}, u32[]{:S(2)}, u32[]{:S(2)}) async-start(bf16[128,2,384]{2,1,0:T(2,128)(2,1)} %all_to_all.58), calls=%async_computation.1 | async-start | bytes 393216 | tf_op jit(solution)/shard_map/all_to_all | solution.py:77
  56.4 506.8 %all-gather.3.cloned.1.call-start = ((), (), s32[]{:S(2)}) async-start(), calls=%async_computation.8 | async-start | bytes 1585152 | tf_op jit(solution)/shard_map/all_gather | solution.py:69
  57.6 32.2 %collective-permute-start.5 = (bf16[256,384]{1,0:T(8,128)(2,1)S(1)}, bf16[256,384]{1,0:T(8,128)(2,1)S(1)}, u32[]{:S(2)}, u32[]{:S(2)}) collective-permute-start(bf16[256,384]{1,0:T(8,128)(2,1)S(1)} %get-tuple-element.24), channel_id=1, source_target_pairs={{0,1},{1,2},{2,3},{3,4},{4,5},{5,6},{6,7},{7,8},{8,9},{9,10},{10,1... | collective-permute-start | bytes 589832 | tf_op jit(solution)/shard_map/ppermute | solution.py:17
  60.5 29.2 %collective-permute-start.4 = (bf16[256,384]{1,0:T(8,128)(2,1)S(1)}, bf16[256,384]{1,0:T(8,128)(2,1)}, u32[]{:S(2)}, u32[]{:S(2)}) collective-permute-start(bf16[256,384]{1,0:T(8,128)(2,1)S(1)} %get-tuple-element.24), channel_id=1, source_target_pairs={{0,2},{1,3},{2,4},{3,5},{4,6},{5,7},{6,8},{7,9},{8,10},{9,11},{10,... | collective-permute-start | bytes 589832 | tf_op jit(solution)/shard_map/ppermute | solution.py:17
  65.0 24.7 %copy-start.6 = (bf16[256,384]{0,1:T(8,128)(2,1)}, bf16[256,384]{0,1:T(8,128)(2,1)S(1)}, u32[]{:S(2)}) copy-start(bf16[256,384]{0,1:T(8,128)(2,1)S(1)} %copy.65) | copy-start | bytes 589828
  68.1 21.6 %collective-permute-start.3 = (bf16[256,384]{1,0:T(8,128)(2,1)S(1)}, bf16[256,384]{1,0:T(8,128)(2,1)}, u32[]{:S(2)}, u32[]{:S(2)}) collective-permute-start(bf16[256,384]{1,0:T(8,128)(2,1)S(1)} %get-tuple-element.24), channel_id=1, source_target_pairs={{0,3},{1,4},{2,5},{3,6},{4,7},{5,8},{6,9},{7,10},{8,11},{9,12},{10... | collective-permute-start | bytes 589832 | tf_op jit(solution)/shard_map/ppermute | solution.py:17
  74.1 28.9 %all-to-all-start.3 = ((bf16[128,2,384]{2,1,0:T(2,128)(2,1)}), bf16[128,2,384]{2,1,0:T(2,128)(2,1)S(1)}, u32[]{:S(2)}, u32[]{:S(2)}) async-start(bf16[128,2,384]{2,1,0:T(2,128)(2,1)} %all_to_all.62), calls=%async_computation.3 | async-start | bytes 393216 | tf_op jit(solution)/shard_map/all_to_all | solution.py:78
  96.0 8.4 copy-start.10
  96.2 8.2 copy-start.9
  104.3 489.3 %copy-start.2 = (f32[8,4,32,32]{2,3,1,0:T(8,128)}, f32[8,4,32,32]{2,3,1,0:T(8,128)S(1)}, u32[]{:S(2)}) copy-start(f32[8,4,32,32]{2,3,1,0:T(8,128)S(1)} %get-tuple-element.33) | copy-start | bytes 393220
  567.7 23.9 %all-to-all-start.2 = ((bf16[128,2,384]{2,1,0:T(2,128)(2,1)}), bf16[128,2,384]{2,1,0:T(2,128)(2,1)}, u32[]{:S(2)}, u32[]{:S(2)}) async-start(bf16[128,2,384]{2,1,0:T(2,128)(2,1)} %all_to_all.60), calls=%async_computation.2 | async-start | bytes 393216 | tf_op jit(solution)/shard_map/all_to_all | solution.py:79
  575.7 3.6 copy-start.1
  575.7 3.6 copy-start.11
  596.9 26.4 %all-to-all-start.7 = ((bf16[128,2,384]{2,1,0:T(2,128)(2,1)}), bf16[128,2,384]{2,1,0:T(2,128)(2,1)}, u32[]{:S(2)}, u32[]{:S(2)}) async-start(bf16[128,2,384]{2,1,0:T(2,128)(2,1)} %all_to_all.73), calls=%async_computation.7 | async-start | bytes 393216 | tf_op jit(solution)/shard_map/all_to_all | solution.py:95
  609.0 84.9 %collective-permute-start.10 = (f32[256,384]{1,0:T(8,128)}, f32[256,384]{1,0:T(8,128)}, u32[]{:S(2)}, u32[]{:S(2)}) collective-permute-start(f32[256,384]{1,0:T(8,128)} %copy.89), channel_id=1, source_target_pairs={{2,0},{3,1},{4,2},{5,3},{6,4},{7,5},{8,6},{9,7},{10,8},{11,9},{12,... | collective-permute-start | bytes 1179656 | tf_op jit(solution)/shard_map/ppermute | solution.py:17
  616.0 4.2 copy-start.3
  616.0 4.2 copy-start.4
  620.2 21.1 %copy-start.5 = (bf16[32,8,4,96]{3,2,1,0:T(4,128)(2,1)S(1)}, bf16[32,8,4,96]{3,2,1,0:T(4,128)(2,1)}, u32[]{:S(2)}) copy-start(bf16[32,8,4,96]{3,2,1,0:T(4,128)(2,1)} %reshape.236) | copy-start | bytes 589828
  623.4 29.1 %all-to-all-start.6 = ((bf16[128,2,384]{2,1,0:T(2,128)(2,1)}), bf16[128,2,384]{2,1,0:T(2,128)(2,1)}, u32[]{:S(2)}, u32[]{:S(2)}) async-start(bf16[128,2,384]{2,1,0:T(2,128)(2,1)} %all_to_all.70), calls=%async_computation.6 | async-start | bytes 393216 | tf_op jit(solution)/shard_map/all_to_all | solution.py:98
  636.5 1187.9 %all-reduce.3.cloned.1.call-start = ((), (), s32[]{:S(2)}) async-start(), calls=%async_computation.9 | async-start | bytes 4718592
  642.6 0.7 copy-start.7
  652.4 47.0 %all-to-all-start.5 = ((bf16[128,2,384]{2,1,0:T(2,128)(2,1)}), bf16[128,2,384]{2,1,0:T(2,128)(2,1)}, u32[]{:S(2)}, u32[]{:S(2)}) async-start(bf16[128,2,384]{2,1,0:T(2,128)(2,1)} %all_to_all.67), calls=%async_computation.5 | async-start | bytes 393216 | tf_op jit(solution)/shard_map/all_to_all | solution.py:97
  664.6 26.8 %copy-start.8 = (bf16[8,4,32,32]{2,3,1,0:T(8,128)(2,1)S(1)}, bf16[8,4,32,32]{2,3,1,0:T(8,128)(2,1)}, u32[]{:S(2)}) copy-start(bf16[8,4,32,32]{2,3,1,0:T(8,128)(2,1)} %copy-done.7) | copy-start | bytes 196612
  675.4 39.1 %collective-permute-start.7 = (f32[256,384]{1,0:T(8,128)}, f32[256,384]{1,0:T(8,128)}, u32[]{:S(2)}, u32[]{:S(2)}) collective-permute-start(f32[256,384]{1,0:T(8,128)} %copy.83), channel_id=1, source_target_pairs={{2,0},{3,1},{4,2},{5,3},{6,4},{7,5},{8,6},{9,7},{10,8},{11,9},{12,... | collective-permute-start | bytes 1179656 | tf_op jit(solution)/shard_map/ppermute | solution.py:17
  682.1 31.1 %collective-permute-start.11 = (f32[256,384]{1,0:T(8,128)}, f32[256,384]{1,0:T(8,128)}, u32[]{:S(2)}, u32[]{:S(2)}) collective-permute-start(f32[256,384]{1,0:T(8,128)} %copy.90), channel_id=1, source_target_pairs={{3,0},{4,1},{5,2},{6,3},{7,4},{8,5},{9,6},{10,7},{11,8},{12,9},{13... | collective-permute-start | bytes 1179656 | tf_op jit(solution)/shard_map/ppermute | solution.py:17
  685.2 28.1 %collective-permute-start.9 = (f32[256,384]{1,0:T(8,128)}, f32[256,384]{1,0:T(8,128)}, u32[]{:S(2)}, u32[]{:S(2)}) collective-permute-start(f32[256,384]{1,0:T(8,128)} %copy.87), channel_id=1, source_target_pairs={{1,0},{2,1},{3,2},{4,3},{5,4},{6,5},{7,6},{8,7},{9,8},{10,9},{11,1... | collective-permute-start | bytes 1179656 | tf_op jit(solution)/shard_map/ppermute | solution.py:17
  689.5 25.1 %collective-permute-start.8 = (f32[256,384]{1,0:T(8,128)}, f32[256,384]{1,0:T(8,128)}, u32[]{:S(2)}, u32[]{:S(2)}) collective-permute-start(f32[256,384]{1,0:T(8,128)} %copy.84), channel_id=1, source_target_pairs={{3,0},{4,1},{5,2},{6,3},{7,4},{8,5},{9,6},{10,7},{11,8},{12,9},{13... | collective-permute-start | bytes 1179656 | tf_op jit(solution)/shard_map/ppermute | solution.py:17
  694.0 20.6 %collective-permute-start.6 = (f32[256,384]{1,0:T(8,128)}, f32[256,384]{1,0:T(8,128)}, u32[]{:S(2)}, u32[]{:S(2)}) collective-permute-start(f32[256,384]{1,0:T(8,128)} %copy.81), channel_id=1, source_target_pairs={{1,0},{2,1},{3,2},{4,3},{5,4},{6,5},{7,6},{8,7},{9,8},{10,9},{11,1... | collective-permute-start | bytes 1179656 | tf_op jit(solution)/shard_map/ppermute | solution.py:17
  699.4 26.8 %all-to-all-start.4 = ((bf16[128,2,384]{2,1,0:T(2,128)(2,1)}), bf16[128,2,384]{2,1,0:T(2,128)(2,1)}, u32[]{:S(2)}, u32[]{:S(2)}) async-start(bf16[128,2,384]{2,1,0:T(2,128)(2,1)} %all_to_all.64), calls=%async_computation.4 | async-start | bytes 393216 | tf_op jit(solution)/shard_map/all_to_all | solution.py:96
Sparse Core Ops, SparseCore 0:
  65.0 498.2 all-gather.2
  641.4 1183.0 all-reduce.2
where the time goes:
time: 1930 us; the launch traced here: 1920 us
  waiting for transfers between devices  1590 us (82%)
  starting transfers between devices  140 us (7%)
  blocking collectives  88.7 us (5%)
  local copies, waits for them, and re-layouts  47.1 us (2%)
  matrix products  26.2 us (1%)
    unnamed x3, waiting for transfers between devices  1090 us
    all_gather x1, waiting for transfers between devices, body(): lax.all_gather(out_weight, 'ctx', axis=0, tiled=True)  459 us
    psum x1, blocking collectives, body(): grad_weight = lax.psum(weight_shard, 'dp')  88.7 us
    ppermute x12, starting transfers between devices, from_behind(): return lax.ppermute(value, axis, pairs)  51 us
  transfers between devices with their start and end apart: 22, of which 8 were waited for; matrix products, arithmetic and copies ran while one was open for 3% of the time, Pallas kernels for 0%

commit v1 on v0

v1 whole, which is shorter than its diff:
```python
import jax
import jax.numpy as jnp
import numpy as np
from jax import lax
from jax.experimental import pallas as pl
from jax.experimental.pallas import tpu as pltpu
from jax.sharding import PartitionSpec as P

HS = 96
HEADS = 4
WIDTH = HEADS * HS
NX, NZ = 4, 16
GROUP = 32
ROWS = 256
CLASSES = 8
SCALE = HS**-0.5
F32, BF16 = jnp.float32, jnp.bfloat16
NT = (((1,), (1,)), ((), ()))
TN = (((0,), (0,)), ((), ()))


def dot(a, b, dims=None):
    if dims is None:
        return jnp.dot(a, b, preferred_element_type=F32)
    return lax.dot_general(a, b, dims, preferred_element_type=F32)


def selections():
    spread = np.zeros((768, 1024), np.float32)
    gather = np.zeros((1024, 768), np.float32)
    for yl in range(2):
        for z in range(NZ):
            for x in range(NX):
                for r in range(6):
                    f = (yl * 64 + z * 4 + x) * 6 + r
                    spread[f, ((yl * 4 + x) * 16 + z) * 8 + r] = 1
                    gather[(((z // 8 * 4 + x) * 2 + yl) * 8 + z % 8) * 8 + r, f] = 1
    pad = np.zeros((WIDTH, 512), np.float32)
    for h in range(HEADS):
        for i in range(HS):
            pad[h * HS + i, h * 128 + i] = 1
    return [jnp.asarray(m, BF16) for m in (spread, gather, pad, pad.T)]


def kernel(
    q_ref, k_ref, v_ref, w_ref, c_ref, spread_ref, gather_ref, pad_ref, unpad_ref,
    gq_ref, gk_ref, gv_ref, gw_ref,
    wz_send, wz_recv, wg, cot_p, cot_t, go,
    cs, cr, qc, kc, vc, dc, probs_ref, half_ref, ds_ref, acc0, acc1,
    rs, rr, rs_do, rr_do, rt_s, rt_r, racc_k, racc_v, att_ref,
    g1_s, g1_r, g_own, g2_s, g2_r, g3_s, g3_r, g4_s, g4_r, g5_s, g5_r,
    ssem, rsem,
):
    dp, ctx = lax.axis_index("dp"), lax.axis_index("ctx")
    core, yh = dp % 2, dp // 2
    x, p = ctx % 4, ctx // 4
    z, yl = p % 16, p // 16
    y = yh * 2 + yl

    def at_p(pp):
        return (dp, pp * 4 + x)

    def at_x(xx):
        return (dp, p * 4 + xx)

    def at_y(yy):
        return ((yy // 2) * 2 + core, (yy % 2) * 64 + z * 4 + x)

    def at_core():
        return (yh * 2 + 1 - core, ctx)

    def send(src, dst, sem, where):
        pltpu.make_async_remote_copy(
            src_ref=src, dst_ref=dst, send_sem=ssem.at[sem], recv_sem=rsem.at[sem],
            device_id=where, device_id_type=pl.DeviceIdType.MESH,
        ).start()

    def take(ref, sem):
        pltpu.make_async_copy(ref, ref, rsem.at[sem]).wait()

    def sent(ref, sem):
        pltpu.make_async_copy(ref, ref, ssem.at[sem]).wait()

    barrier = pltpu.get_barrier_semaphore()

    def greet(where):
        pl.semaphore_signal(barrier, inc=1, device_id=where, device_id_type=pl.DeviceIdType.MESH)

    def greet_p(i, _):
        greet(at_p((p + i) % GROUP))
        return 0

    lax.fori_loop(1, GROUP, greet_p, 0)
    for i in range(1, 4):
        greet(at_x((x + i) % 4))
        greet(at_y((y + i) % 4))
    greet(at_core())
    greet(((1 - yh) * 2 + 1 - core, ctx))

    def pack(slot, a_ref, a0, b_ref, b0):
        def one(m, _):
            rows = pl.ds(pl.multiple_of(m * 16, 16), 16)
            a = a_ref[rows, a0 : a0 + WIDTH].astype(F32)
            b = b_ref[rows, b0 : b0 + WIDTH].astype(F32)
            cs[slot, 2 * m] = jnp.concatenate([a[:8], b[:8]], 0).astype(BF16)
            cs[slot, 2 * m + 1] = jnp.concatenate([a[8:], b[8:]], 0).astype(BF16)
            return 0

        lax.fori_loop(0, 16, one, 0)

    def exchange(slot):
        def one(i, _):
            half = (i + 1) // 2
            ahead = (i % 2) * half + (1 - i % 2) * (GROUP - half)
            pp = (p + ahead) % GROUP
            send(cs.at[slot, pp], cr.at[slot, p], slot, at_p(pp))
            return 0

        lax.fori_loop(1, GROUP, one, 0)
        cr[slot, p] = cs[slot, p]

    def arrived(slot):
        take(cr.at[slot, pl.ds(0, GROUP - 1)], slot)

    def unpack(slot, a_ref, a0, b_ref, b0):
        def one(m, _):
            rows = pl.ds(pl.multiple_of(m * 16, 16), 16)
            first = cr[slot, 2 * m].astype(F32)
            second = cr[slot, 2 * m + 1].astype(F32)
            a_ref[rows, a0 : a0 + WIDTH] = jnp.concatenate([first[:8], second[:8]], 0).astype(BF16)
            b_ref[rows, b0 : b0 + WIDTH] = jnp.concatenate([first[8:], second[8:]], 0).astype(BF16)
            return 0

        lax.fori_loop(0, 16, one, 0)

    w = w_ref[...].astype(F32)
    wz_send[...] = jnp.zeros((8, WIDTH), F32)
    wz_send[0:6, :] = jnp.where(core == 0, w[:, :WIDTH], w[:, WIDTH:])
    wz_recv[z] = wz_send[...]
    pack(0, q_ref, WIDTH, k_ref, WIDTH)
    pl.semaphore_wait(barrier, 39)

    def send_w(i, _):
        zz = (z + i) % NZ
        send(wz_send, wz_recv.at[z], 4, at_p(yl * 16 + zz))
        return 0

    lax.fori_loop(1, NZ, send_w, 0)
    exchange(0)

    for index, ref in enumerate((q_ref, k_ref, v_ref)):
        padded = dot(ref[:, :WIDTH], pad_ref[...]).astype(BF16)
        for h in range(HEADS):
            rs[h, index] = padded[:, h * 128 : (h + 1) * 128]
    for i in range(1, 4):
        xx = (x + i) % 4
        send(rs.at[xx], rr.at[x], 5, at_x(xx))
    rr[x] = rs[x]

    cot_p[...] = dot(c_ref[...], spread_ref[...]).astype(BF16)
    cot_t[...] = dot(gather_ref[...], c_ref[...], NT).astype(BF16)

    take(wz_recv.at[pl.ds(0, NZ - 1)], 4)
    wg[core, yl * 4 + x] = wz_recv[...].reshape(128, WIDTH).astype(BF16)
    own = wg.at[core, yl * 4 + x]
    for i in range(1, 4):
        send(own, own, 6, at_x((x + i) % 4))
    mine = wg.at[core, pl.ds(yl * 4, 4)]
    take(wg.at[core, pl.ds(yl * 4, 3)], 6)
    for i, first in ((1, 0), (3, 2)):
        part = wg.at[core, pl.ds(yl * 4 + first, 2)]
        send(part, part, 7, at_y((y + i) % 4))
    send(mine, mine, 8, at_core())
    other = wg.at[core, pl.ds((1 - yl) * 4, 4)]
    take(other, 7)
    send(other, other, 9, at_core())
    take(wg.at[1 - core, pl.ds(yl * 4, 4)], 8)
    take(wg.at[1 - core, pl.ds((1 - yl) * 4, 4)], 9)
    for c in range(2):
        go[:, c * WIDTH : (c + 1) * WIDTH] = dot(
            cot_p[...], wg[c].reshape(1024, WIDTH)
        ).astype(BF16)

    pack(1, v_ref, WIDTH, go, WIDTH)
    exchange(1)
    padded = dot(go[:, :WIDTH], pad_ref[...]).astype(BF16)
    for h in range(HEADS):
        rs_do[h] = padded[:, h * 128 : (h + 1) * 128]
    for i in range(1, 4):
        xx = (x + i) % 4
        send(rs_do.at[xx], rr_do.at[x], 10, at_x(xx))
    rr_do[x] = rs_do[x]

    arrived(0)
    unpack(0, qc, 0, kc, 0)
    row_at = lax.broadcasted_iota(jnp.int32, (ROWS, ROWS), 0)
    key_at = lax.broadcasted_iota(jnp.int32, (ROWS, ROWS), 1)
    lanes = lax.broadcasted_iota(jnp.int32, (ROWS, WIDTH), 1)

    def span(h):
        return h * HS // 128 * 128, -(-(h + 1) * HS // 128) * 128

    def head(ref, h):
        lo, hi = span(h)
        at = lanes[:, lo:hi]
        value = ref[:, lo:hi]
        return jnp.where((at >= h * HS) & (at < (h + 1) * HS), value, jnp.zeros_like(value))

    def softmax(scores):
        top = jnp.max(scores, axis=1, keepdims=True)
        total = top + jnp.log(jnp.sum(jnp.exp(scores - top), axis=1, keepdims=True))
        return jnp.exp(scores - total)

    for h in range(HEADS):
        lo, hi = span(h)
        scores = dot(head(qc, h), kc[:, lo:hi], NT) * SCALE
        allowed = (key_at <= row_at) & ((row_at - key_at) % CLASSES == 0)
        probs = softmax(jnp.where(allowed, scores, -1e30))
        probs_ref[h] = probs
        half_ref[h] = probs.astype(BF16)

    take(rr.at[pl.ds(0, 3)], 5)
    take(rr_do.at[pl.ds(0, 3)], 10)
    racc_k[...] = jnp.zeros_like(racc_k)
    racc_v[...] = jnp.zeros_like(racc_v)
    for i in range(4):
        n = (i + 1) * ROWS
        query, out = rr[i, 0], rr_do[i]
        keys = rr[0 : i + 1, 1].reshape(n, 128)
        values = rr[0 : i + 1, 2].reshape(n, 128)
        at = lax.broadcasted_iota(jnp.int32, (ROWS, n), 0) + i * ROWS
        allowed = lax.broadcasted_iota(jnp.int32, (ROWS, n), 1) <= at
        probs = softmax(jnp.where(allowed, dot(query, keys, NT) * SCALE, -1e30))
        half = probs.astype(BF16)
        attended = dot(half, values).astype(BF16)
        deltas = jnp.sum(out.astype(F32) * attended.astype(F32), axis=1, keepdims=True)
        dscores = (probs * (dot(out, values, NT) - deltas) * SCALE).astype(BF16)
        rt_s[i, 0] = attended
        rt_s[i, 1] = dot(dscores, keys).astype(BF16)
        racc_k[0:n, :] += dot(dscores, query, TN)
        racc_v[0:n, :] += dot(half, out, TN)
    for i in range(4):
        rt_s[i, 2] = racc_k[i * ROWS : (i + 1) * ROWS, :].astype(BF16)
        rt_s[i, 3] = racc_v[i * ROWS : (i + 1) * ROWS, :].astype(BF16)
    for i in range(1, 4):
        xx = (x + i) % 4
        send(rt_s.at[xx], rt_r.at[x], 11, at_x(xx))
    rt_r[x] = rt_s[x]

    arrived(1)
    unpack(1, vc, 0, dc, 0)
    acc0[...] = jnp.zeros_like(acc0)
    acc1[...] = jnp.zeros_like(acc1)
    for h in range(HEADS):
        lo, hi = span(h)
        out = head(dc, h)
        attended = dot(half_ref[h], head(vc, h))
        acc0[:, lo:hi] += attended
        deltas = jnp.sum(out.astype(F32) * attended.astype(BF16).astype(F32), axis=1, keepdims=True)
        dprobs = dot(out, vc[:, lo:hi], NT)
        dscores = (probs_ref[h] * (dprobs - deltas) * SCALE).astype(BF16)
        ds_ref[h] = dscores
        acc1[:, lo:hi] += dot(dscores, head(kc, h))
    pack(2, acc0, 0, acc1, 0)
    exchange(2)
    acc0[...] = jnp.zeros_like(acc0)
    acc1[...] = jnp.zeros_like(acc1)
    for h in range(HEADS):
        lo, hi = span(h)
        acc0[:, lo:hi] += dot(ds_ref[h], head(qc, h), TN)
        acc1[:, lo:hi] += dot(half_ref[h], head(dc, h), TN)
    pack(3, acc0, 0, acc1, 0)
    exchange(3)

    def reduce_core(g):
        attended = att_ref[:, g * WIDTH : (g + 1) * WIDTH]
        theirs = pl.ds(pl.multiple_of((1 - core) * 512, 512), 512)
        ours = pl.ds(pl.multiple_of(core * 512, 512), 512)
        g1_s[g] = dot(cot_t[theirs, :], attended).astype(BF16)
        send(g1_s.at[g], g1_r.at[g], 12 + g, at_core())
        g_own[g] = dot(cot_t[ours, :], attended).reshape(4, 128, WIDTH)

    def reduce_x(g):
        take(g1_r.at[g], 12 + g)
        total = g_own[g] + g1_r[g].astype(F32).reshape(4, 128, WIDTH)
        g_own[g] = total
        g2_s[g] = total.astype(BF16)
        for i in range(1, 4):
            xx = (x + i) % 4
            send(g2_s.at[g, xx], g2_r.at[g, i - 1], 14 + g, at_x(xx))

    def reduce_y(g):
        take(g2_r.at[g], 14 + g)
        total = g_own[g, x]
        for i in range(3):
            total = total + g2_r[g, i].astype(F32)
        g3_s[g] = total.reshape(4, 32, WIDTH)
        for i in range(1, 4):
            yy = (y + i) % 4
            send(g3_s.at[g, (yy % 2) * 2 + yy // 2], g3_r.at[g, i - 1], 16 + g, at_y(yy))

    def reduce_z(g):
        take(g3_r.at[g], 16 + g)
        total = g3_s[g, yl * 2 + yh]
        for i in range(3):
            total = total + g3_r[g, i]
        g4_s[g] = total.reshape(4, 8, WIDTH)
        for i in range(4):
            zz = core * 8 + yh * 4 + i

            @pl.when(zz != z)
            def _():
                send(g4_s.at[g, i], g4_r.at[g, z], 18 + g, at_p(yl * 16 + zz))

    owner = (z // 8 == core) & (z // 4 % 2 == yh)

    def reduce_last(g):
        @pl.when(owner)
        def _():
            take(g4_r.at[g, pl.ds(0, NZ - 1)], 18 + g)
            g4_r[g, z] = g4_s[g, z % 4]
            g5_s[g] = jnp.sum(g4_r[g], axis=0)
            for c in (1, 2, 3):
                send(g5_s.at[g], g5_r.at[g], 20 + g, ((dp + c) % 4, ctx))

    def finish(g):
        @pl.when(owner)
        def _():
            gw_ref[:, g * WIDTH : (g + 1) * WIDTH] = g5_s[g, 0:6, :]

        @pl.when(jnp.logical_not(owner))
        def _():
            take(g5_r.at[g], 20 + g)
            gw_ref[:, g * WIDTH : (g + 1) * WIDTH] = g5_r[g, 0:6, :]

    take(rt_r.at[pl.ds(0, 3)], 11)
    for index, ref in enumerate((att_ref, gq_ref, gk_ref, gv_ref)):
        heads = jnp.concatenate([rt_r[h, index] for h in range(HEADS)], axis=1)
        ref[:, :WIDTH] = dot(heads, unpad_ref[...]).astype(BF16)
    reduce_core(0)
    reduce_x(0)
    reduce_y(0)
    arrived(2)
    unpack(2, att_ref, WIDTH, gq_ref, WIDTH)
    reduce_core(1)
    reduce_z(0)
    reduce_x(1)
    reduce_y(1)
    reduce_last(0)
    reduce_z(1)
    arrived(3)
    unpack(3, gk_ref, WIDTH, gv_ref, WIDTH)
    reduce_last(1)
    finish(0)
    finish(1)

    for slot in range(4):
        sent(cs.at[slot, pl.ds(0, GROUP - 1)], slot)
    sent(wz_recv.at[pl.ds(0, NZ - 1)], 4)
    sent(rs.at[pl.ds(0, 3)], 5)
    sent(wg.at[core, pl.ds(0, 3)], 6)
    sent(mine, 7)
    sent(mine, 8)
    sent(other, 9)
    sent(rs_do.at[pl.ds(0, 3)], 10)
    sent(rt_s.at[pl.ds(0, 3)], 11)
    for g in range(2):
        sent(g1_s.at[g], 12 + g)
        sent(g2_s.at[g, pl.ds(0, 3)], 14 + g)
        sent(g3_s.at[g, pl.ds(0, 3)], 16 + g)
        quarter = (z // 8 == core) & (z // 4 % 2 == yh)

        @pl.when(quarter)
        def _():
            sent(g4_s.at[g, pl.ds(0, 3)], 18 + g)
            sent(g4_s.at[g, pl.ds(0, 3)], 20 + g)

        @pl.when(jnp.logical_not(quarter))
        def _():
            sent(g4_s.at[g], 18 + g)


def body(queries, key_rows, value_rows, out_weight, cotangent, *matrices):
    vmem = pl.BlockSpec(memory_space=pltpu.VMEM)
    tokens = jax.ShapeDtypeStruct((ROWS, 2 * WIDTH), BF16)
    outs = pl.pallas_call(
        kernel,
        out_shape=(tokens, tokens, tokens, jax.ShapeDtypeStruct((6, 2 * WIDTH), F32)),
        in_specs=[vmem] * 9,
        out_specs=(vmem,) * 4,
        scratch_shapes=[
            pltpu.VMEM((8, WIDTH), F32),
            pltpu.VMEM((NZ, 8, WIDTH), F32),
            pltpu.VMEM((2, 8, 128, WIDTH), BF16),
            pltpu.VMEM((ROWS, 1024), BF16),
            pltpu.VMEM((1024, ROWS), BF16),
            pltpu.VMEM((ROWS, 2 * WIDTH), BF16),
            pltpu.VMEM((4, GROUP, 16, WIDTH), BF16),
            pltpu.VMEM((4, GROUP, 16, WIDTH), BF16),
            pltpu.VMEM((ROWS, WIDTH), BF16),
            pltpu.VMEM((ROWS, WIDTH), BF16),
            pltpu.VMEM((ROWS, WIDTH), BF16),
            pltpu.VMEM((ROWS, WIDTH), BF16),
            pltpu.VMEM((HEADS, ROWS, ROWS), F32),
            pltpu.VMEM((HEADS, ROWS, ROWS), BF16),
            pltpu.VMEM((HEADS, ROWS, ROWS), BF16),
            pltpu.VMEM((ROWS, WIDTH), F32),
            pltpu.VMEM((ROWS, WIDTH), F32),
            pltpu.VMEM((4, 3, ROWS, 128), BF16),
            pltpu.VMEM((4, 3, ROWS, 128), BF16),
            pltpu.VMEM((4, ROWS, 128), BF16),
            pltpu.VMEM((4, ROWS, 128), BF16),
            pltpu.VMEM((4, 4, ROWS, 128), BF16),
            pltpu.VMEM((4, 4, ROWS, 128), BF16),
            pltpu.VMEM((1024, 128), F32),
            pltpu.VMEM((1024, 128), F32),
            pltpu.VMEM((ROWS, 2 * WIDTH), BF16),
            pltpu.VMEM((2, 512, WIDTH), BF16),
            pltpu.VMEM((2, 512, WIDTH), BF16),
            pltpu.VMEM((2, 4, 128, WIDTH), F32),
            pltpu.VMEM((2, 4, 128, WIDTH), BF16),
            pltpu.VMEM((2, 3, 128, WIDTH), BF16),
            pltpu.VMEM((2, 4, 32, WIDTH), F32),
            pltpu.VMEM((2, 3, 32, WIDTH), F32),
            pltpu.VMEM((2, 4, 8, WIDTH), F32),
            pltpu.VMEM((2, NZ, 8, WIDTH), F32),
            pltpu.VMEM((2, 8, WIDTH), F32),
            pltpu.VMEM((2, 8, WIDTH), F32),
            pltpu.SemaphoreType.DMA((22,)),
            pltpu.SemaphoreType.DMA((22,)),
        ],
        compiler_params=pltpu.CompilerParams(
            collective_id=0, has_side_effects=True, vmem_limit_bytes=56 * 1024 * 1024
        ),
        cost_estimate=pl.CostEstimate(
            flops=8_000_000_000, bytes_accessed=8_000_000, transcendentals=2_000_000
        ),
        name="strided_attention",
    )(queries[0], key_rows[0], value_rows[0], out_weight, cotangent[0], *matrices)
    return (outs[0][None], outs[1][None], outs[2][None], outs[3])


def solution(mesh):
    tokens, rows = P("dp", "ctx", None), P("ctx", None)
    matrices = selections()
    mapped = jax.shard_map(
        body,
        mesh=mesh,
        in_specs=(tokens, tokens, tokens, rows, tokens) + (P(None, None),) * len(matrices),
        out_specs=(tokens, tokens, tokens, rows),
        check_vma=False,
    )

    def run(queries, key_rows, value_rows, out_weight, cotangent):
        return mapped(queries, key_rows, value_rows, out_weight, cotangent, *matrices)

    return run
```

time: 1930 us -> 124 us (0.06)
  waiting for transfers between devices: 1590 us -> 0 us
  starting transfers between devices: 140 us -> 0 us
  Pallas kernels: 0 us -> 118 us
  blocking collectives: 88.7 us -> 0 us
  local copies, waits for them, and re-layouts: 47.1 us -> 4.94 us
  matrix products: 26.2 us -> 0 us
    unnamed x3 -> x0, waiting for transfers between devices: 1090 us -> none
    all_gather x1 -> x0, waiting for transfers between devices: 459 us -> none  [body(): lax.all_gather(out_weight, 'ctx', axis=0, tiled=True)]
    pallas_call x0 -> x1, Pallas kernels: none -> 118 us  [body(): pl.pallas_call(kernel, out_shape=(tokens, tokens, tokens, jax.ShapeDtypeS...]
    all_to_all x8 -> x0, starting transfers between devices: 88.8 us -> none  [the longest x1 20.1 us: body(): lax.all_to_all(query_all[:, row_width:], 'ctx', split_axis=0, concat_axis...]
    psum x1 -> x0, blocking collectives: 88.7 us -> none  [body(): grad_weight = lax.psum(weight_shard, 'dp')]
    ppermute x12 -> x0, starting transfers between devices: 51 us -> none  [from_behind(): return lax.ppermute(value, axis, pairs)]
    all_to_all x8 -> x0, waiting for transfers between devices: 39.7 us -> none  [the longest x1 8.77 us: body(): lax.all_to_all(grad_out[:, row_width:], 'ctx', split_axis=0, concat_axis=...]
    dot_general x14 -> x0, matrix products: 26.2 us -> none  [the longest x2 5.67 us: softmax_parts(): jnp.einsum('hqk,khd->qhd', probs_half, value_heads, preferred_element_typ...]
  transfers between devices with their start and end apart: 22 -> 0, of which waited for: 8 -> 0; matrix products, arithmetic and copies ran while one was open for 3% -> 0% of each run, Pallas kernels for 0% -> 0%
where the time goes in v1:
time: 124 us
  Pallas kernels  118 us (95%)
  local copies, waits for them, and re-layouts  4.94 us (4%)
    pallas_call x1, Pallas kernels, body(): pl.pallas_call(kernel, out_shape=(tokens, tokens, tokens, jax.ShapeDtypeS...  118 us
    unnamed x8, local copies, waits for them, and re-layouts  4.94 us

profile of v1, /device:TPU:25, one launch (start us, length us, event | category | flops | bytes accessed | tf_op | source)
XLA Modules:
  0.0 124.1 jit_solution(10449365427896407695)
XLA Ops:
  0.6 118.5 %strided_attention.1 = (bf16[256,768]{1,0:T(8,128)(2,1)}, bf16[256,768]{1,0:T(8,128)(2,1)}, bf16[256,768]{1,0:T(8,128)(2,1)}, f32[6,768]{1,0:T(8,128)}) custom-call(bf16[256,768]{1,0:T(8,128)(2,1)} %bitcast.10, bf16[256,768]{1,0:T(8,128)(2,1)} %bitcast.11, bf16[256,768]{1,0:T(8,128)(2,1)} %bitcast.12, bf16[6,768]{1,0:T(8,128)(2,1)} %w_ref.1, ...), custom_call_target="tpu_custom_call" | custom-call | flops 8000000000 | bytes 8000000 | tf_op jit(solution)/shard_map/strided_attention/pallas_call | solution.py:386
  119.1 0.0 copy-start
  119.1 0.0 copy-start.1
  119.1 1.8 %copy.17 = bf16[1,256,768]{2,1,0:T(8,128)(2,1)} copy(bf16[1,256,768]{2,1,0:T(8,128)(2,1)} %bitcast.9) | data formatting | bytes 786432
  120.9 1.8 %copy.18 = bf16[1,256,768]{2,1,0:T(8,128)(2,1)} copy(bf16[1,256,768]{2,1,0:T(8,128)(2,1)} %bitcast.8) | data formatting | bytes 786432
  122.7 0.0 copy-done
  122.7 0.7 copy.19
  123.4 0.0 copy-done.1
  123.5 0.6 copy.20
Async XLA Ops:
  119.1 3.6 %copy-start = (bf16[256,768]{1,0:T(8,128)(2,1)S(1)}, bf16[256,768]{1,0:T(8,128)(2,1)}, u32[]{:S(2)}) copy-start(bf16[256,768]{1,0:T(8,128)(2,1)} %get-tuple-element.10) | copy-start | bytes 1179652
  119.1 4.3 %copy-start.1 = (f32[6,768]{1,0:T(8,128)S(1)}, f32[6,768]{1,0:T(8,128)}, u32[]{:S(2)}) copy-start(f32[6,768]{1,0:T(8,128)} %get-tuple-element.19) | copy-start | bytes 55300

commit v2 on v1

v2 whole, which is shorter than its diff:
```python
import jax
import jax.numpy as jnp
import numpy as np
from jax import lax
from jax.experimental import pallas as pl
from jax.experimental.pallas import tpu as pltpu
from jax.sharding import PartitionSpec as P

HS = 96
HEADS = 4
WIDTH = HEADS * HS
NX, NZ = 4, 16
GROUP = 32
ROWS = 256
CLASSES = 8
SCALE = HS**-0.5
F32, BF16 = jnp.float32, jnp.bfloat16
NT = (((1,), (1,)), ((), ()))
TN = (((0,), (0,)), ((), ()))


def dot(a, b, dims=None):
    if dims is None:
        return jnp.dot(a, b, preferred_element_type=F32)
    return lax.dot_general(a, b, dims, preferred_element_type=F32)


def selections():
    spread = np.zeros((768, 768), np.float32)
    gather = np.zeros((1024, 768), np.float32)
    for yl in range(2):
        for z in range(NZ):
            for x in range(NX):
                for r in range(6):
                    f = (yl * 64 + z * 4 + x) * 6 + r
                    spread[f, (((r // 3 * 2 + yl) * 4 + x) * 16 + z) * 3 + r % 3] = 1
                    gather[(((z // 8 * 4 + x) * 2 + yl) * 8 + z % 8) * 8 + r, f] = 1
    rows = np.zeros((3, 48, 256), np.float32)
    for t in range(3):
        for z in range(NZ):
            for r in range(3):
                rows[t, z * 3 + r, z * 16 + r * 3 + t] = 1
    pad = np.zeros((WIDTH, 512), np.float32)
    for h in range(HEADS):
        for i in range(HS):
            pad[h * HS + i, h * 128 + i] = 1
    return [jnp.asarray(m, BF16) for m in (spread, gather, rows, pad, pad.T)]


WZ, WX, WY, WC, RQ, RD, RT, G1, G2, G3, G4, G5 = 7, 8, 9, 12, 16, 17, 18, 19, 21, 23, 25, 27
SEMS = 29
TILES = (3, 2, 1, 1, 1, 2, 2)


def kernel(
    q_hbm, k_hbm, v_hbm, w_hbm, c_hbm, spread_hbm, gather_hbm, rows_hbm, pad_hbm, unpad_hbm,
    gq_ref, gk_ref, gv_ref, gw_ref,
    q_ref, k_ref, v_ref, w_ref, c_ref, spread_ref, gather_ref, rows_ref, pad_ref, unpad_ref,
    wz_rows, wz_send, wz_recv, wg, cot_p, cot_t, go,
    cs0, cs1, cs2, cs3, cs4, cs5, cs6, cr0, cr1, cr2, cr3, cr4, cr5, cr6,
    qc, kc, vc, dc, probs_ref, half_ref, ds_ref, att_a, dq_a, dk_a, dv_a,
    rs, rr, rs_do, rr_do, rt_s, rt_r, racc_k, racc_v, att_ref,
    g1_s, g1_r, g_own, g2_s, g2_r, g3_s, g3_r, g3_own, g4_s, g4_r, g5_s, g5_r,
    isem, ssem, rsem,
):
    cs, cr = (cs0, cs1, cs2, cs3, cs4, cs5, cs6), (cr0, cr1, cr2, cr3, cr4, cr5, cr6)
    dp, ctx = lax.axis_index("dp"), lax.axis_index("ctx")
    core, yh = lax.rem(dp, 2), lax.div(dp, 2)
    x, p = lax.rem(ctx, 4), lax.div(ctx, 4)
    z, yl = lax.rem(p, 16), lax.div(p, 16)
    y = yh * 2 + yl

    loads = [
        pltpu.make_async_copy(src, dst, isem.at[i])
        for i, (src, dst) in enumerate(
            (
                (q_hbm, q_ref), (k_hbm, k_ref), (w_hbm, w_ref), (v_hbm, v_ref), (pad_hbm, pad_ref),
                (c_hbm, c_ref), (spread_hbm, spread_ref), (rows_hbm, rows_ref),
                (gather_hbm, gather_ref), (unpad_hbm, unpad_ref),
            )
        )
    ]
    (load_q, load_k, load_w, load_v, load_pad, load_c, load_spread, load_rows, load_gather,
     load_unpad) = loads
    for load in loads[:3]:
        load.start()

    def at_p(pp):
        return (dp, pp * 4 + x)

    def at_x(xx):
        return (dp, p * 4 + xx)

    def at_y(yy):
        return (lax.div(yy, 2) * 2 + core, lax.rem(yy, 2) * 64 + z * 4 + x)

    def at_core():
        return (yh * 2 + 1 - core, ctx)

    def ring(i, by, n):
        return lax.rem(i + by, n)

    def send(src, dst, sem, where):
        pltpu.make_async_remote_copy(
            src_ref=src, dst_ref=dst, send_sem=ssem.at[sem], recv_sem=rsem.at[sem],
            device_id=where, device_id_type=pl.DeviceIdType.MESH,
        ).start()

    def take(ref, sem):
        pltpu.make_async_copy(ref, ref, rsem.at[sem]).wait()

    def sent(ref, sem):
        pltpu.make_async_copy(ref, ref, ssem.at[sem]).wait()

    barrier = pltpu.get_barrier_semaphore()

    def greet(where):
        pl.semaphore_signal(barrier, inc=1, device_id=where, device_id_type=pl.DeviceIdType.MESH)

    def greet_p(i, _):
        greet(at_p(ring(p, i, GROUP)))
        return 0

    lax.fori_loop(1, GROUP, greet_p, 0)
    for i in range(1, 4):
        greet(at_x(ring(x, i, 4)))
        greet(at_y(ring(y, i, 4)))
    greet(at_core())
    greet(((1 - yh) * 2 + 1 - core, ctx))
    for load in loads[3:]:
        load.start()

    def pack(slot, pairs):
        def one(m, _):
            rows = pl.ds(pl.multiple_of(m * 16, 16), 16)
            for t, ((a_ref, a0), (b_ref, b0)) in enumerate(pairs):
                a = a_ref[rows, a0 : a0 + 128].astype(F32)
                b = b_ref[rows, b0 : b0 + 128].astype(F32)
                lanes = slice(t * 128, (t + 1) * 128)
                cs[slot][2 * m, :, lanes] = jnp.concatenate([a[:8], b[:8]], 0).astype(BF16)
                cs[slot][2 * m + 1, :, lanes] = jnp.concatenate([a[8:], b[8:]], 0).astype(BF16)
            return 0

        lax.fori_loop(0, 16, one, 0)

    def exchange(slot):
        def one(i, _):
            half = lax.div(i + 1, 2)
            odd = lax.rem(i, 2)
            pp = ring(p, odd * half + (1 - odd) * (GROUP - half), GROUP)
            send(cs[slot].at[pp], cr[slot].at[p], slot, at_p(pp))
            return 0

        lax.fori_loop(1, GROUP, one, 0)
        cr[slot][p] = cs[slot][p]

    def unpack(slot, pairs):
        take(cr[slot].at[pl.ds(0, GROUP - 1)], slot)

        def one(m, _):
            rows = pl.ds(pl.multiple_of(m * 16, 16), 16)
            for t, ((a_ref, a0), (b_ref, b0)) in enumerate(pairs):
                lanes = slice(t * 128, (t + 1) * 128)
                first = cr[slot][2 * m, :, lanes].astype(F32)
                second = cr[slot][2 * m + 1, :, lanes].astype(F32)
                a_ref[rows, a0 : a0 + 128] = jnp.concatenate([first[:8], second[:8]], 0).astype(BF16)
                b_ref[rows, b0 : b0 + 128] = jnp.concatenate([first[8:], second[8:]], 0).astype(BF16)
            return 0

        lax.fori_loop(0, 16, one, 0)

    load_q.wait()
    load_k.wait()
    pack(0, [((q_ref, WIDTH + t), (k_ref, WIDTH + t)) for t in (0, 128, 256)])
    load_w.wait()
    w = w_ref[...].astype(F32)
    w = jnp.where(core == 0, w[:, :WIDTH], w[:, WIDTH:])
    w = jnp.where(yh == 0, w[0:3], w[3:6])
    wz_rows[...] = jnp.zeros((16, 128), F32)
    for r in range(3):
        for t in range(3):
            wz_rows[r * 3 + t : r * 3 + t + 1, :] = w[r : r + 1, t * 128 : (t + 1) * 128]
    wz_send[...] = wz_rows[...].astype(BF16)
    wz_recv[z] = wz_send[...]
    pl.semaphore_wait(barrier, 39)

    def send_w(i, _):
        send(wz_send, wz_recv.at[z], WZ, at_p(yl * 16 + ring(z, i, NZ)))
        return 0

    lax.fori_loop(1, NZ, send_w, 0)
    exchange(0)

    load_pad.wait()
    load_v.wait()
    for index, ref in enumerate((q_ref, k_ref, v_ref)):
        padded = dot(ref[:, :WIDTH], pad_ref[...]).astype(BF16)
        for h in range(HEADS):
            rs[h, index] = padded[:, h * 128 : (h + 1) * 128]
    for i in range(1, 4):
        xx = ring(x, i, 4)
        send(rs.at[xx], rr.at[x], RQ, at_x(xx))
    rr[x] = rs[x]

    load_rows.wait()
    take(wz_recv.at[pl.ds(0, NZ - 1)], WZ)
    gathered = wz_recv[...].reshape(256, 128)
    at = yl * 4 + x
    for t in range(3):
        wg[core, yh, at, :, t * 128 : (t + 1) * 128] = dot(rows_ref[t], gathered).astype(BF16)
    own = wg.at[core, yh, at]
    for i in range(1, 4):
        send(own, own, WX, at_x(ring(x, i, 4)))

    load_c.wait()
    load_spread.wait()
    cot_p[...] = dot(c_ref[...], spread_ref[...]).astype(BF16)

    mine = wg.at[core, yh, pl.ds(yl * 4, 4)]
    take(wg.at[core, yh, pl.ds(0, 3)], WX)
    for i in (1, 3, 2):
        send(mine, mine, WY + i - 1, at_y(ring(y, i, 4)))
    send(mine, mine, WC, at_core())
    load_gather.wait()
    cot_t[...] = dot(gather_ref[...], c_ref[...], NT).astype(BF16)
    for i in (1, 3, 2):
        yy = ring(y, 4 - i, 4)
        part = wg.at[core, lax.div(yy, 2), pl.ds(lax.rem(yy, 2) * 4, 4)]
        take(part, WY + i - 1)
        send(part, part, WC + i, at_core())
    for i in range(4):
        take(mine, WC + i)

    def grad_out(c):
        go[:, c * WIDTH : (c + 1) * WIDTH] = dot(
            cot_p[...], wg[c].reshape(768, WIDTH)
        ).astype(BF16)

    grad_out(1)
    pack(1, [((v_ref, WIDTH + t), (go, WIDTH + t)) for t in (0, 128)])
    exchange(1)
    pack(2, [((v_ref, WIDTH + 256), (go, WIDTH + 256))])
    exchange(2)
    grad_out(0)
    padded = dot(go[:, :WIDTH], pad_ref[...]).astype(BF16)
    for h in range(HEADS):
        rs_do[h] = padded[:, h * 128 : (h + 1) * 128]
    for i in range(1, 4):
        xx = ring(x, i, 4)
        send(rs_do.at[xx], rr_do.at[x], RD, at_x(xx))
    rr_do[x] = rs_do[x]

    unpack(0, [((qc, t), (kc, t)) for t in (0, 128, 256)])
    row_at = lax.broadcasted_iota(jnp.int32, (ROWS, ROWS), 0)
    key_at = lax.broadcasted_iota(jnp.int32, (ROWS, ROWS), 1)
    lanes = lax.broadcasted_iota(jnp.int32, (ROWS, WIDTH), 1)

    def span(h):
        return h * HS // 128 * 128, -(-(h + 1) * HS // 128) * 128

    def head(ref, h):
        lo, hi = span(h)
        at = lanes[:, lo:hi]
        value = ref[:, lo:hi]
        return jnp.where((at >= h * HS) & (at < (h + 1) * HS), value, jnp.zeros_like(value))

    def put(ref, h, value):
        lo, hi = span(h)
        for t in range(lo, hi, 128):
            if h > 0 and t == lo:
                ref[:, t : t + 128] += value[:, t - lo : t - lo + 128]
            else:
                ref[:, t : t + 128] = value[:, t - lo : t - lo + 128]

    def softmax(scores):
        top = jnp.max(scores, axis=1, keepdims=True)
        total = top + jnp.log(jnp.sum(jnp.exp(scores - top), axis=1, keepdims=True))
        return jnp.exp(scores - total)

    for h in range(HEADS):
        lo, hi = span(h)
        scores = dot(head(qc, h), kc[:, lo:hi], NT) * SCALE
        allowed = (key_at <= row_at) & (lax.rem(row_at - key_at, CLASSES) == 0)
        probs = softmax(jnp.where(allowed, scores, -1e30))
        probs_ref[h] = probs
        half_ref[h] = probs.astype(BF16)

    take(rr.at[pl.ds(0, 3)], RQ)
    take(rr_do.at[pl.ds(0, 3)], RD)
    racc_k[...] = jnp.zeros_like(racc_k)
    racc_v[...] = jnp.zeros_like(racc_v)
    for i in range(4):
        n = (i + 1) * ROWS
        query, out = rr[i, 0], rr_do[i]
        keys = rr[0 : i + 1, 1].reshape(n, 128)
        values = rr[0 : i + 1, 2].reshape(n, 128)
        at = lax.broadcasted_iota(jnp.int32, (ROWS, n), 0) + i * ROWS
        allowed = lax.broadcasted_iota(jnp.int32, (ROWS, n), 1) <= at
        probs = softmax(jnp.where(allowed, dot(query, keys, NT) * SCALE, -1e30))
        half = probs.astype(BF16)
        attended = dot(half, values).astype(BF16)
        deltas = jnp.sum(out.astype(F32) * attended.astype(F32), axis=1, keepdims=True)
        dscores = (probs * (dot(out, values, NT) - deltas) * SCALE).astype(BF16)
        rt_s[i, 0] = attended
        rt_s[i, 1] = dot(dscores, keys).astype(BF16)
        racc_k[0:n, :] += dot(dscores, query, TN)
        racc_v[0:n, :] += dot(half, out, TN)
    for i in range(4):
        rt_s[i, 2] = racc_k[i * ROWS : (i + 1) * ROWS, :].astype(BF16)
        rt_s[i, 3] = racc_v[i * ROWS : (i + 1) * ROWS, :].astype(BF16)
    for i in range(1, 4):
        xx = ring(x, i, 4)
        send(rt_s.at[xx], rt_r.at[x], RT, at_x(xx))
    rt_r[x] = rt_s[x]

    def attend(h):
        put(att_a, h, dot(half_ref[h], head(vc, h)).astype(BF16).astype(F32))

    def score_grads(h):
        lo, hi = span(h)
        out = head(dc, h)
        deltas = jnp.sum(out.astype(F32) * att_a[:, lo:hi], axis=1, keepdims=True)
        dprobs = dot(out, vc[:, lo:hi], NT)
        dscores = (probs_ref[h] * (dprobs - deltas) * SCALE).astype(BF16)
        ds_ref[h] = dscores
        put(dq_a, h, dot(dscores, head(kc, h)))

    def key_grads(h):
        put(dk_a, h, dot(ds_ref[h], head(qc, h), TN))
        put(dv_a, h, dot(half_ref[h], head(dc, h), TN))

    unpack(1, [((vc, t), (dc, t)) for t in (0, 128)])
    for h in (0, 1):
        attend(h)
        score_grads(h)
    pack(3, [((att_a, 0), (dq_a, 0))])
    exchange(3)
    for h in (0, 1):
        key_grads(h)
    unpack(2, [((vc, 256), (dc, 256))])
    for h in (2, 3):
        attend(h)
    pack(4, [((att_a, 128), (att_a, 256))])
    exchange(4)
    for h in (2, 3):
        score_grads(h)
    pack(5, [((dk_a, 0), (dv_a, 0)), ((dq_a, 128), (dq_a, 256))])
    exchange(5)
    for h in (2, 3):
        key_grads(h)
    pack(6, [((dk_a, 128), (dk_a, 256)), ((dv_a, 128), (dv_a, 256))])
    exchange(6)

    def reduce_core(g):
        attended = att_ref[:, g * WIDTH : (g + 1) * WIDTH]
        theirs = pl.ds(pl.multiple_of((1 - core) * 512, 512), 512)
        ours = pl.ds(pl.multiple_of(core * 512, 512), 512)
        g1_s[g] = dot(cot_t[theirs, :], attended).astype(BF16)
        send(g1_s.at[g], g1_r.at[g], G1 + g, at_core())
        g_own[g] = dot(cot_t[ours, :], attended).reshape(4, 128, WIDTH)

    def reduce_x(g):
        take(g1_r.at[g], G1 + g)
        total = g_own[g] + g1_r[g].astype(F32).reshape(4, 128, WIDTH)
        g_own[g] = total
        g2_s[g] = total.astype(BF16)
        for i in (1, 3, 2):
            xx = ring(x, i, 4)
            send(g2_s.at[g, xx], g2_r.at[g, i - 1], G2 + g, at_x(xx))

    def reduce_y(g):
        take(g2_r.at[g], G2 + g)
        total = g_own[g, x]
        for i in range(3):
            total = total + g2_r[g, i].astype(F32)
        g3_own[g] = total.reshape(4, 32, WIDTH)
        g3_s[g] = total.reshape(4, 32, WIDTH).astype(BF16)
        for i in (1, 3, 2):
            yy = ring(y, i, 4)
            send(g3_s.at[g, lax.rem(yy, 2) * 2 + lax.div(yy, 2)], g3_r.at[g, i - 1], G3 + g, at_y(yy))

    def reduce_z(g):
        take(g3_r.at[g], G3 + g)
        total = g3_own[g, yl * 2 + yh]
        for i in range(3):
            total = total + g3_r[g, i].astype(F32)
        g4_s[g] = total.reshape(4, 8, WIDTH)
        for i in range(4):
            zz = core * 8 + yh * 4 + i

            @pl.when(zz != z)
            def _():
                send(g4_s.at[g, i], g4_r.at[g, z], G4 + g, at_p(yl * 16 + zz))

    owner = (lax.div(z, 8) == core) & (lax.rem(lax.div(z, 4), 2) == yh)

    def reduce_last(g):
        @pl.when(owner)
        def _():
            take(g4_r.at[g, pl.ds(0, NZ - 1)], G4 + g)
            g4_r[g, z] = g4_s[g, lax.rem(z, 4)]
            g5_s[g] = jnp.sum(g4_r[g], axis=0)
            for c in (1, 2, 3):
                send(g5_s.at[g], g5_r.at[g], G5 + g, (ring(dp, c, 4), ctx))

    def finish(g):
        @pl.when(owner)
        def _():
            gw_ref[:, g * WIDTH : (g + 1) * WIDTH] = g5_s[g, 0:6, :]

        @pl.when(jnp.logical_not(owner))
        def _():
            take(g5_r.at[g], G5 + g)
            gw_ref[:, g * WIDTH : (g + 1) * WIDTH] = g5_r[g, 0:6, :]

    load_unpad.wait()
    take(rt_r.at[pl.ds(0, 3)], RT)
    for index, ref in enumerate((att_ref, gq_ref, gk_ref, gv_ref)):
        heads = jnp.concatenate([rt_r[h, index] for h in range(HEADS)], axis=1)
        ref[:, :WIDTH] = dot(heads, unpad_ref[...]).astype(BF16)
    reduce_core(0)
    reduce_x(0)
    unpack(3, [((att_ref, WIDTH), (gq_ref, WIDTH))])
    reduce_y(0)
    unpack(4, [((att_ref, WIDTH + 128), (att_ref, WIDTH + 256))])
    reduce_core(1)
    reduce_z(0)
    reduce_x(1)
    reduce_y(1)
    reduce_last(0)
    reduce_z(1)
    finish(0)
    unpack(5, [((gk_ref, WIDTH), (gv_ref, WIDTH)), ((gq_ref, WIDTH + 128), (gq_ref, WIDTH + 256))])
    reduce_last(1)
    finish(1)
    unpack(6, [((gk_ref, WIDTH + 128), (gk_ref, WIDTH + 256)), ((gv_ref, WIDTH + 128), (gv_ref, WIDTH + 256))])

    for slot in range(7):
        sent(cs[slot].at[pl.ds(0, GROUP - 1)], slot)
    sent(wz_recv.at[pl.ds(0, NZ - 1)], WZ)
    sent(rs.at[pl.ds(0, 3)], RQ)
    sent(wg.at[core, yh, pl.ds(0, 3)], WX)
    for i in range(3):
        sent(mine, WY + i)
    for i in range(4):
        sent(mine, WC + i)
    sent(rs_do.at[pl.ds(0, 3)], RD)
    sent(rt_s.at[pl.ds(0, 3)], RT)
    for g in range(2):
        sent(g1_s.at[g], G1 + g)
        sent(g2_s.at[g, pl.ds(0, 3)], G2 + g)
        sent(g3_s.at[g, pl.ds(0, 3)], G3 + g)

        @pl.when(owner)
        def _():
            sent(g4_s.at[g, pl.ds(0, 3)], G4 + g)
            sent(g4_s.at[g, pl.ds(0, 3)], G5 + g)

        @pl.when(jnp.logical_not(owner))
        def _():
            sent(g4_s.at[g], G4 + g)


def hand_over(*refs):
    half = len(refs) // 2
    for src, dst in zip(refs[:half], refs[half:], strict=True):
        dst[...] = src[...].reshape(dst.shape)


def body(queries, key_rows, value_rows, out_weight, cotangent, *matrices):
    vmem, hbm = pl.BlockSpec(memory_space=pltpu.VMEM), pl.BlockSpec(memory_space=pl.ANY)
    tokens = jax.ShapeDtypeStruct((ROWS, 2 * WIDTH), BF16)
    weight = jax.ShapeDtypeStruct((6, 2 * WIDTH), F32)
    inputs = (queries[0], key_rows[0], value_rows[0], out_weight, cotangent[0], *matrices)
    messages = [pltpu.VMEM((GROUP, 16, 128 * t), BF16) for t in TILES]
    outs = pl.pallas_call(
        kernel,
        out_shape=(tokens, tokens, tokens, weight),
        in_specs=[hbm] * len(inputs),
        out_specs=(vmem,) * 4,
        scratch_shapes=[pltpu.VMEM(a.shape, a.dtype) for a in inputs]
        + [
            pltpu.VMEM((16, 128), F32),
            pltpu.VMEM((16, 128), BF16),
            pltpu.VMEM((NZ, 16, 128), BF16),
            pltpu.VMEM((2, 2, 8, 48, WIDTH), BF16),
            pltpu.VMEM((ROWS, 768), BF16),
            pltpu.VMEM((1024, ROWS), BF16),
            pltpu.VMEM((ROWS, 2 * WIDTH), BF16),
            *messages,
            *messages,
            pltpu.VMEM((ROWS, WIDTH), BF16),
            pltpu.VMEM((ROWS, WIDTH), BF16),
            pltpu.VMEM((ROWS, WIDTH), BF16),
            pltpu.VMEM((ROWS, WIDTH), BF16),
            pltpu.VMEM((HEADS, ROWS, ROWS), F32),
            pltpu.VMEM((HEADS, ROWS, ROWS), BF16),
            pltpu.VMEM((HEADS, ROWS, ROWS), BF16),
            pltpu.VMEM((ROWS, WIDTH), F32),
            pltpu.VMEM((ROWS, WIDTH), F32),
            pltpu.VMEM((ROWS, WIDTH), F32),
            pltpu.VMEM((ROWS, WIDTH), F32),
            pltpu.VMEM((4, 3, ROWS, 128), BF16),
            pltpu.VMEM((4, 3, ROWS, 128), BF16),
            pltpu.VMEM((4, ROWS, 128), BF16),
            pltpu.VMEM((4, ROWS, 128), BF16),
            pltpu.VMEM((4, 4, ROWS, 128), BF16),
            pltpu.VMEM((4, 4, ROWS, 128), BF16),
            pltpu.VMEM((1024, 128), F32),
            pltpu.VMEM((1024, 128), F32),
            pltpu.VMEM((ROWS, 2 * WIDTH), BF16),
            pltpu.VMEM((2, 512, WIDTH), BF16),
            pltpu.VMEM((2, 512, WIDTH), BF16),
            pltpu.VMEM((2, 4, 128, WIDTH), F32),
            pltpu.VMEM((2, 4, 128, WIDTH), BF16),
            pltpu.VMEM((2, 3, 128, WIDTH), BF16),
            pltpu.VMEM((2, 4, 32, WIDTH), BF16),
            pltpu.VMEM((2, 3, 32, WIDTH), BF16),
            pltpu.VMEM((2, 4, 32, WIDTH), F32),
            pltpu.VMEM((2, 4, 8, WIDTH), F32),
            pltpu.VMEM((2, NZ, 8, WIDTH), F32),
            pltpu.VMEM((2, 8, WIDTH), F32),
            pltpu.VMEM((2, 8, WIDTH), F32),
            pltpu.SemaphoreType.DMA((len(inputs),)),
            pltpu.SemaphoreType.DMA((SEMS,)),
            pltpu.SemaphoreType.DMA((SEMS,)),
        ],
        compiler_params=pltpu.CompilerParams(
            collective_id=0, has_side_effects=True, vmem_limit_bytes=48 * 1024 * 1024
        ),
        cost_estimate=pl.CostEstimate(
            flops=8_000_000_000, bytes_accessed=8_000_000, transcendentals=2_000_000
        ),
        name="strided_attention",
    )(*inputs)
    whole = jax.ShapeDtypeStruct((1, ROWS, 2 * WIDTH), BF16)
    return pl.pallas_call(
        hand_over,
        out_shape=(whole, whole, whole, weight),
        in_specs=[vmem] * 4,
        out_specs=(vmem,) * 4,
        name="hand_over",
    )(*outs)


def solution(mesh):
    tokens, rows = P("dp", "ctx", None), P("ctx", None)
    matrices = selections()
    mapped = jax.shard_map(
        body,
        mesh=mesh,
        in_specs=(tokens, tokens, tokens, rows, tokens) + (P(None, None),) * len(matrices),
        out_specs=(tokens, tokens, tokens, rows),
        check_vma=False,
    )

    def run(queries, key_rows, value_rows, out_weight, cotangent):
        return mapped(queries, key_rows, value_rows, out_weight, cotangent, *matrices)

    return run
```

time: 124 us -> 124 us (level)
  Pallas kernels: 118 us -> 111 us
  local copies, waits for them, and re-layouts: 4.94 us -> 11.7 us
    pallas_call x1 -> x2, Pallas kernels: 118 us -> 111 us  [the longest x1 109 us: body(): pl.pallas_call(kernel, out_shape=(tokens, tokens, tokens, weight), in_spe...]
    unnamed x8 -> x26, local copies, waits for them, and re-layouts: 4.94 us -> 11.7 us
where the time goes in v2:
time: 124 us; the launch traced here: 123 us
  Pallas kernels  111 us (90%)
  local copies, waits for them, and re-layouts  11.7 us (9%)
    pallas_call x1, Pallas kernels, body(): pl.pallas_call(kernel, out_shape=(tokens, tokens, tokens, weight), in_spe...  109 us
    unnamed x26, local copies, waits for them, and re-layouts  11.7 us

profile of v2, /device:TPU:25, one launch (start us, length us, event | category | flops | bytes accessed | tf_op | source)
XLA Modules:
  0.0 123.1 jit_solution(430118415191854584)
XLA Ops:
  0.6 0.0 copy-start.4
  0.6 1.0 copy-done.4
  1.6 0.0 copy-start.5
  1.6 1.0 copy-done.5
  2.6 0.0 copy-start.6
  2.6 1.0 copy-done.6
  3.6 0.0 copy-start.7
  3.6 1.0 copy-done.7
  4.6 0.0 copy-start.8
  4.6 0.7 copy-done.8
  5.3 0.0 copy-start.9
  5.3 1.3 %copy-done.9 = bf16[768,768]{1,0:T(8,128)(2,1)S(1)} copy-done((bf16[768,768]{1,0:T(8,128)(2,1)S(1)}, bf16[768,768]{1,0:T(8,128)(2,1)}, u32[]{:S(2)}) %copy-start.9) | copy-done | bytes 1179672
  6.6 0.0 copy-start.10
  6.6 1.0 copy-done.10
  7.6 0.0 copy-start.11
  7.6 1.0 copy-done.11
  8.6 0.0 copy-start.12
  8.6 0.9 copy-done.12
  9.5 108.5 %strided_attention.1 = (bf16[256,768]{1,0:T(8,128)(2,1)S(1)}, bf16[256,768]{1,0:T(8,128)(2,1)S(1)}, bf16[256,768]{1,0:T(8,128)(2,1)S(1)}, f32[6,768]{1,0:T(8,128)S(1)}) custom-call(bf16[256,768]{1,0:T(8,128)(2,1)S(1)} %bitcast.4, bf16[256,768]{1,0:T(8,128)(2,1)S(1)} %bitcast.5, bf16[256,768]{1,0:T(8,128)(2,1)S(1)} %bitcast.6, bf16[6,768]{1,0:T(8,128)(2,1)S(1)} %copy-done.8, ...), custom_call_target="tpu_custom_call" | custom-call | flops 8000000000 | bytes 8000000 | tf_op jit(solution)/shard_map/strided_attention/pallas_call | solution.py:476
  118.0 0.0 copy-start
  118.0 0.7 copy-done
  118.7 0.0 copy-start.1
  118.7 0.7 copy-done.1
  119.5 0.0 copy-start.2
  119.5 0.7 copy-done.2
  120.2 0.0 copy-start.3
  120.2 0.6 copy-done.3
  120.8 2.3 %hand_over.1 = (bf16[1,256,768]{2,1,0:T(8,128)(2,1)}, bf16[1,256,768]{2,1,0:T(8,128)(2,1)}, bf16[1,256,768]{2,1,0:T(8,128)(2,1)}, f32[6,768]{1,0:T(8,128)}) custom-call(bf16[256,768]{1,0:T(8,128)(2,1)} %copy-done, bf16[256,768]{1,0:T(8,128)(2,1)} %copy-done.1, bf16[256,768]{1,0:T(8,128)(2,1)} %copy-done.2, f32[6,768]{1,0:T(8,128)} %copy-done.3), custom_call_target="tpu_custom_call" | custom-call | tf_op jit(solution)/shard_map/hand_over/pallas_call | solution.py:537
Async XLA Ops:
  0.6 1.0 copy-start.4
  1.6 1.0 copy-start.5
  2.6 1.0 copy-start.6
  3.6 1.0 copy-start.7
  4.6 0.7 copy-start.8
  5.3 1.3 %copy-start.9 = (bf16[768,768]{1,0:T(8,128)(2,1)S(1)}, bf16[768,768]{1,0:T(8,128)(2,1)}, u32[]{:S(2)}) copy-start(bf16[768,768]{1,0:T(8,128)(2,1)} %constant.10.clone.spread_hbm) | copy-start | bytes 3538948
  6.6 1.0 copy-start.10
  7.6 1.0 copy-start.11
  8.6 0.9 copy-start.12
  118.0 0.7 copy-start
  118.7 0.7 copy-start.1
  119.5 0.7 copy-start.2
  120.2 0.6 copy-start.3

commit v3 on v2

--- a/solution.py
+++ b/solution.py
@@ -47,9 +47,9 @@
     return [jnp.asarray(m, BF16) for m in (spread, gather, rows, pad, pad.T)]
 
 
-WZ, WX, WY, WC, RQ, RD, RT, G1, G2, G3, G4, G5 = 7, 8, 9, 12, 16, 17, 18, 19, 21, 23, 25, 27
-SEMS = 29
-TILES = (3, 2, 1, 1, 1, 2, 2)
+WZ, WX, WY, WC, RQ, RD, RT, G1, G2, G3, G4 = 8, 9, 10, 13, 17, 18, 19, 20, 22, 24, 25
+SEMS = 26
+TILES = (4, 1, 1, 1, 1, 2, 1, 1)
 
 
 def kernel(
@@ -57,32 +57,34 @@
     gq_ref, gk_ref, gv_ref, gw_ref,
     q_ref, k_ref, v_ref, w_ref, c_ref, spread_ref, gather_ref, rows_ref, pad_ref, unpad_ref,
     wz_rows, wz_send, wz_recv, wg, cot_p, cot_t, go,
-    cs0, cs1, cs2, cs3, cs4, cs5, cs6, cr0, cr1, cr2, cr3, cr4, cr5, cr6,
+    cs0, cs1, cs2, cs3, cs4, cs5, cs6, cs7, cr0, cr1, cr2, cr3, cr4, cr5, cr6, cr7,
     qc, kc, vc, dc, probs_ref, half_ref, ds_ref, att_a, dq_a, dk_a, dv_a,
     rs, rr, rs_do, rr_do, rt_s, rt_r, racc_k, racc_v, att_ref,
-    g1_s, g1_r, g_own, g2_s, g2_r, g3_s, g3_r, g3_own, g4_s, g4_r, g5_s, g5_r,
+    g1_s, g1_r, g_own, g2_s, g2_r, g_sum, g3_s, g3_r, g4_s, g4_r,
     isem, ssem, rsem,
 ):
-    cs, cr = (cs0, cs1, cs2, cs3, cs4, cs5, cs6), (cr0, cr1, cr2, cr3, cr4, cr5, cr6)
+    cs = (cs0, cs1, cs2, cs3, cs4, cs5, cs6, cs7)
+    cr = (cr0, cr1, cr2, cr3, cr4, cr5, cr6, cr7)
     dp, ctx = lax.axis_index("dp"), lax.axis_index("ctx")
     core, yh = lax.rem(dp, 2), lax.div(dp, 2)
     x, p = lax.rem(ctx, 4), lax.div(ctx, 4)
     z, yl = lax.rem(p, 16), lax.div(p, 16)
     y = yh * 2 + yl
+    chunk = x * 4 + yl * 2 + yh
 
     loads = [
         pltpu.make_async_copy(src, dst, isem.at[i])
         for i, (src, dst) in enumerate(
             (
-                (q_hbm, q_ref), (k_hbm, k_ref), (w_hbm, w_ref), (v_hbm, v_ref), (pad_hbm, pad_ref),
+                (q_hbm, q_ref), (k_hbm, k_ref), (v_hbm, v_ref), (w_hbm, w_ref), (pad_hbm, pad_ref),
                 (c_hbm, c_ref), (spread_hbm, spread_ref), (rows_hbm, rows_ref),
                 (gather_hbm, gather_ref), (unpad_hbm, unpad_ref),
             )
         )
     ]
-    (load_q, load_k, load_w, load_v, load_pad, load_c, load_spread, load_rows, load_gather,
+    (load_q, load_k, load_v, load_w, load_pad, load_c, load_spread, load_rows, load_gather,
      load_unpad) = loads
-    for load in loads[:3]:
+    for load in loads[:4]:
         load.start()
 
     def at_p(pp):
@@ -93,6 +95,9 @@
 
     def at_y(yy):
         return (lax.div(yy, 2) * 2 + core, lax.rem(yy, 2) * 64 + z * 4 + x)
+
+    def at_chunk(c):
+        return (lax.rem(c, 2) * 2 + core, lax.rem(lax.div(c, 2), 2) * 64 + z * 4 + lax.div(c, 4))
 
     def at_core():
         return (yh * 2 + 1 - core, ctx)
@@ -122,12 +127,16 @@
         return 0
 
     lax.fori_loop(1, GROUP, greet_p, 0)
-    for i in range(1, 4):
-        greet(at_x(ring(x, i, 4)))
-        greet(at_y(ring(y, i, 4)))
+
+
+    def greet_chunk(i, _):
+        greet(at_chunk(ring(chunk, i, 16)))
+        return 0
+
+    lax.fori_loop(1, 16, greet_chunk, 0)
     greet(at_core())
     greet(((1 - yh) * 2 + 1 - core, ctx))
-    for load in loads[3:]:
+    for load in loads[4:]:
         load.start()
 
     def pack(slot, pairs):
@@ -171,7 +180,12 @@
 
     load_q.wait()
     load_k.wait()
-    pack(0, [((q_ref, WIDTH + t), (k_ref, WIDTH + t)) for t in (0, 128, 256)])
+    load_v.wait()
+    pack(
+        0,
+        [((q_ref, WIDTH + t), (k_ref, WIDTH + t)) for t in (0, 128, 256)]
+        + [((v_ref, WIDTH), (v_ref, WIDTH + 128))],
+    )
     load_w.wait()
     w = w_ref[...].astype(F32)
     w = jnp.where(core == 0, w[:, :WIDTH], w[:, WIDTH:])
@@ -182,7 +196,7 @@
             wz_rows[r * 3 + t : r * 3 + t + 1, :] = w[r : r + 1, t * 128 : (t + 1) * 128]
     wz_send[...] = wz_rows[...].astype(BF16)
     wz_recv[z] = wz_send[...]
-    pl.semaphore_wait(barrier, 39)
+    pl.semaphore_wait(barrier, 48)
 
     def send_w(i, _):
         send(wz_send, wz_recv.at[z], WZ, at_p(yl * 16 + ring(z, i, NZ)))
@@ -192,7 +206,6 @@
     exchange(0)
 
     load_pad.wait()
-    load_v.wait()
     for index, ref in enumerate((q_ref, k_ref, v_ref)):
         padded = dot(ref[:, :WIDTH], pad_ref[...]).astype(BF16)
         for h in range(HEADS):
@@ -204,8 +217,8 @@
 
     load_rows.wait()
     take(wz_recv.at[pl.ds(0, NZ - 1)], WZ)
+    at = yl * 4 + x
     gathered = wz_recv[...].reshape(256, 128)
-    at = yl * 4 + x
     for t in range(3):
         wg[core, yh, at, :, t * 128 : (t + 1) * 128] = dot(rows_ref[t], gathered).astype(BF16)
     own = wg.at[core, yh, at]
@@ -237,9 +250,9 @@
         ).astype(BF16)
 
     grad_out(1)
-    pack(1, [((v_ref, WIDTH + t), (go, WIDTH + t)) for t in (0, 128)])
+    pack(1, [((go, WIDTH), (go, WIDTH + 128))])
     exchange(1)
-    pack(2, [((v_ref, WIDTH + 256), (go, WIDTH + 256))])
+    pack(2, [((go, WIDTH + 256), (v_ref, WIDTH + 256))])
     exchange(2)
     grad_out(0)
     padded = dot(go[:, :WIDTH], pad_ref[...]).astype(BF16)
@@ -250,7 +263,7 @@
         send(rs_do.at[xx], rr_do.at[x], RD, at_x(xx))
     rr_do[x] = rs_do[x]
 
-    unpack(0, [((qc, t), (kc, t)) for t in (0, 128, 256)])
+    unpack(0, [((qc, t), (kc, t)) for t in (0, 128, 256)] + [((vc, 0), (vc, 128))])
     row_at = lax.broadcasted_iota(jnp.int32, (ROWS, ROWS), 0)
     key_at = lax.broadcasted_iota(jnp.int32, (ROWS, ROWS), 1)
     lanes = lax.broadcasted_iota(jnp.int32, (ROWS, WIDTH), 1)
@@ -329,7 +342,7 @@
         put(dk_a, h, dot(ds_ref[h], head(qc, h), TN))
         put(dv_a, h, dot(half_ref[h], head(dc, h), TN))
 
-    unpack(1, [((vc, t), (dc, t)) for t in (0, 128)])
+    unpack(1, [((dc, 0), (dc, 128))])
     for h in (0, 1):
         attend(h)
         score_grads(h)
@@ -337,7 +350,7 @@
     exchange(3)
     for h in (0, 1):
         key_grads(h)
-    unpack(2, [((vc, 256), (dc, 256))])
+    unpack(2, [((dc, 256), (vc, 256))])
     for h in (2, 3):
         attend(h)
     pack(4, [((att_a, 128), (att_a, 256))])
@@ -348,8 +361,9 @@
     exchange(5)
     for h in (2, 3):
         key_grads(h)
-    pack(6, [((dk_a, 128), (dk_a, 256)), ((dv_a, 128), (dv_a, 256))])
+    pack(6, [((dk_a, 128), (dk_a, 256))])
     exchange(6)
+    pack(7, [((dv_a, 128), (dv_a, 256))])
 
     def reduce_core(g):
         attended = att_ref[:, g * WIDTH : (g + 1) * WIDTH]
@@ -357,61 +371,62 @@
         ours = pl.ds(pl.multiple_of(core * 512, 512), 512)
         g1_s[g] = dot(cot_t[theirs, :], attended).astype(BF16)
         send(g1_s.at[g], g1_r.at[g], G1 + g, at_core())
-        g_own[g] = dot(cot_t[ours, :], attended).reshape(4, 128, WIDTH)
-
-    def reduce_x(g):
+        g_own[g] = dot(cot_t[ours, :], attended).reshape(16, 32, WIDTH)
+
+    def reduce_plane(g):
         take(g1_r.at[g], G1 + g)
-        total = g_own[g] + g1_r[g].astype(F32).reshape(4, 128, WIDTH)
+        total = g_own[g] + g1_r[g].astype(F32).reshape(16, 32, WIDTH)
         g_own[g] = total
         g2_s[g] = total.astype(BF16)
-        for i in (1, 3, 2):
-            xx = ring(x, i, 4)
-            send(g2_s.at[g, xx], g2_r.at[g, i - 1], G2 + g, at_x(xx))
-
-    def reduce_y(g):
-        take(g2_r.at[g], G2 + g)
-        total = g_own[g, x]
-        for i in range(3):
-            total = total + g2_r[g, i].astype(F32)
-        g3_own[g] = total.reshape(4, 32, WIDTH)
-        g3_s[g] = total.reshape(4, 32, WIDTH).astype(BF16)
-        for i in (1, 3, 2):
-            yy = ring(y, i, 4)
-            send(g3_s.at[g, lax.rem(yy, 2) * 2 + lax.div(yy, 2)], g3_r.at[g, i - 1], G3 + g, at_y(yy))
-
-    def reduce_z(g):
-        take(g3_r.at[g], G3 + g)
-        total = g3_own[g, yl * 2 + yh]
-        for i in range(3):
-            total = total + g3_r[g, i].astype(F32)
-        g4_s[g] = total.reshape(4, 8, WIDTH)
+
+        def one(i, _):
+            c = ring(chunk, i, 16)
+            send(g2_s.at[g, c], g2_r.at[g, chunk], G2 + g, at_chunk(c))
+            return 0
+
+        lax.fori_loop(1, 16, one, 0)
+        g2_r[g, chunk] = jnp.zeros((32, WIDTH), BF16)
+
+    def reduce_z():
+        for g in range(2):
+            take(g2_r.at[g, pl.ds(0, 15)], G2 + g)
+            total = g_own[g, chunk]
+            for c in range(16):
+                total = total + g2_r[g, c].astype(F32)
+            g_sum[g] = total.reshape(4, 8, WIDTH)
         for i in range(4):
             zz = core * 8 + yh * 4 + i
+            g3_s[i] = jnp.concatenate([g_sum[0, i], g_sum[1, i]], 0).astype(BF16)
 
             @pl.when(zz != z)
             def _():
-                send(g4_s.at[g, i], g4_r.at[g, z], G4 + g, at_p(yl * 16 + zz))
+                send(g3_s.at[i], g3_r.at[z], G3, at_p(yl * 16 + zz))
 
     owner = (lax.div(z, 8) == core) & (lax.rem(lax.div(z, 4), 2) == yh)
 
-    def reduce_last(g):
+    def reduce_last():
         @pl.when(owner)
         def _():
-            take(g4_r.at[g, pl.ds(0, NZ - 1)], G4 + g)
-            g4_r[g, z] = g4_s[g, lax.rem(z, 4)]
-            g5_s[g] = jnp.sum(g4_r[g], axis=0)
+            take(g3_r.at[pl.ds(0, NZ - 1)], G3)
+            g3_r[z] = g3_s[lax.rem(z, 4)]
+            total = g3_r[0].astype(F32)
+            for i in range(1, NZ):
+                total = total + g3_r[i].astype(F32)
+            g4_s[...] = total
             for c in (1, 2, 3):
-                send(g5_s.at[g], g5_r.at[g], G5 + g, (ring(dp, c, 4), ctx))
-
-    def finish(g):
+                send(g4_s, g4_r, G4, (ring(dp, c, 4), ctx))
+
+    def finish():
         @pl.when(owner)
         def _():
-            gw_ref[:, g * WIDTH : (g + 1) * WIDTH] = g5_s[g, 0:6, :]
+            g4_r[...] = g4_s[...]
 
         @pl.when(jnp.logical_not(owner))
         def _():
-            take(g5_r.at[g], G5 + g)
-            gw_ref[:, g * WIDTH : (g + 1) * WIDTH] = g5_r[g, 0:6, :]
+            take(g4_r, G4)
+
+        gw_ref[:, :WIDTH] = g4_r[0:6, :]
+        gw_ref[:, WIDTH:] = g4_r[8:14, :]
 
     load_unpad.wait()
     take(rt_r.at[pl.ds(0, 3)], RT)
@@ -419,23 +434,20 @@
         heads = jnp.concatenate([rt_r[h, index] for h in range(HEADS)], axis=1)
         ref[:, :WIDTH] = dot(heads, unpad_ref[...]).astype(BF16)
     reduce_core(0)
-    reduce_x(0)
     unpack(3, [((att_ref, WIDTH), (gq_ref, WIDTH))])
-    reduce_y(0)
     unpack(4, [((att_ref, WIDTH + 128), (att_ref, WIDTH + 256))])
     reduce_core(1)
-    reduce_z(0)
-    reduce_x(1)
-    reduce_y(1)
-    reduce_last(0)
-    reduce_z(1)
-    finish(0)
+    reduce_plane(0)
+    reduce_plane(1)
+    reduce_z()
+    exchange(7)
     unpack(5, [((gk_ref, WIDTH), (gv_ref, WIDTH)), ((gq_ref, WIDTH + 128), (gq_ref, WIDTH + 256))])
-    reduce_last(1)
-    finish(1)
-    unpack(6, [((gk_ref, WIDTH + 128), (gk_ref, WIDTH + 256)), ((gv_ref, WIDTH + 128), (gv_ref, WIDTH + 256))])
-
-    for slot in range(7):
+    reduce_last()
+    unpack(6, [((gk_ref, WIDTH + 128), (gk_ref, WIDTH + 256))])
+    finish()
+    unpack(7, [((gv_ref, WIDTH + 128), (gv_ref, WIDTH + 256))])
+
+    for slot in range(8):
         sent(cs[slot].at[pl.ds(0, GROUP - 1)], slot)
     sent(wz_recv.at[pl.ds(0, NZ - 1)], WZ)
     sent(rs.at[pl.ds(0, 3)], RQ)
@@ -448,27 +460,34 @@
     sent(rt_s.at[pl.ds(0, 3)], RT)
     for g in range(2):
         sent(g1_s.at[g], G1 + g)
-        sent(g2_s.at[g, pl.ds(0, 3)], G2 + g)
-        sent(g3_s.at[g, pl.ds(0, 3)], G3 + g)
-
-        @pl.when(owner)
-        def _():
-            sent(g4_s.at[g, pl.ds(0, 3)], G4 + g)
-            sent(g4_s.at[g, pl.ds(0, 3)], G5 + g)
-
-        @pl.when(jnp.logical_not(owner))
-        def _():
-            sent(g4_s.at[g], G4 + g)
+        sent(g2_s.at[g, pl.ds(0, 15)], G2 + g)
+
+    @pl.when(owner)
+    def _():
+        sent(g3_s.at[pl.ds(0, 3)], G3)
+        sent(g_sum.at[pl.ds(0, 2), pl.ds(0, 3)], G4)
+
+    @pl.when(jnp.logical_not(owner))
+    def _():
+        sent(g3_s, G3)
 
 
 def hand_over(*refs):
-    half = len(refs) // 2
-    for src, dst in zip(refs[:half], refs[half:], strict=True):
-        dst[...] = src[...].reshape(dst.shape)
+    n = 4
+    srcs, dsts, held, sems = refs[:n], refs[n : 2 * n], refs[2 * n : 3 * n], refs[3 * n]
+    inward = [pltpu.make_async_copy(a, b, sems.at[0, i]) for i, (a, b) in enumerate(zip(srcs, held, strict=True))]
+    outward = [pltpu.make_async_copy(a, b, sems.at[1, i]) for i, (a, b) in enumerate(zip(held, dsts, strict=True))]
+    for copy in inward:
+        copy.start()
+    for first, second in zip(inward, outward, strict=True):
+        first.wait()
+        second.start()
+    for copy in outward:
+        copy.wait()
 
 
 def body(queries, key_rows, value_rows, out_weight, cotangent, *matrices):
-    vmem, hbm = pl.BlockSpec(memory_space=pltpu.VMEM), pl.BlockSpec(memory_space=pl.ANY)
+    vmem, hbm = pl.BlockSpec(memory_space=pltpu.VMEM), pl.BlockSpec(memory_space=pltpu.HBM)
     tokens = jax.ShapeDtypeStruct((ROWS, 2 * WIDTH), BF16)
     weight = jax.ShapeDtypeStruct((6, 2 * WIDTH), F32)
     inputs = (queries[0], key_rows[0], value_rows[0], out_weight, cotangent[0], *matrices)
@@ -511,36 +530,35 @@
             pltpu.VMEM((ROWS, 2 * WIDTH), BF16),
             pltpu.VMEM((2, 512, WIDTH), BF16),
             pltpu.VMEM((2, 512, WIDTH), BF16),
-            pltpu.VMEM((2, 4, 128, WIDTH), F32),
-            pltpu.VMEM((2, 4, 128, WIDTH), BF16),
-            pltpu.VMEM((2, 3, 128, WIDTH), BF16),
-            pltpu.VMEM((2, 4, 32, WIDTH), BF16),
-            pltpu.VMEM((2, 3, 32, WIDTH), BF16),
-            pltpu.VMEM((2, 4, 32, WIDTH), F32),
+            pltpu.VMEM((2, 16, 32, WIDTH), F32),
+            pltpu.VMEM((2, 16, 32, WIDTH), BF16),
+            pltpu.VMEM((2, 16, 32, WIDTH), BF16),
             pltpu.VMEM((2, 4, 8, WIDTH), F32),
-            pltpu.VMEM((2, NZ, 8, WIDTH), F32),
-            pltpu.VMEM((2, 8, WIDTH), F32),
-            pltpu.VMEM((2, 8, WIDTH), F32),
+            pltpu.VMEM((4, 16, WIDTH), BF16),
+            pltpu.VMEM((NZ, 16, WIDTH), BF16),
+            pltpu.VMEM((16, WIDTH), F32),
+            pltpu.VMEM((16, WIDTH), F32),
             pltpu.SemaphoreType.DMA((len(inputs),)),
             pltpu.SemaphoreType.DMA((SEMS,)),
             pltpu.SemaphoreType.DMA((SEMS,)),
         ],
         compiler_params=pltpu.CompilerParams(
-            collective_id=0, has_side_effects=True, vmem_limit_bytes=48 * 1024 * 1024
+            collective_id=0, has_side_effects=True, vmem_limit_bytes=60 * 1024 * 1024
         ),
         cost_estimate=pl.CostEstimate(
             flops=8_000_000_000, bytes_accessed=8_000_000, transcendentals=2_000_000
         ),
         name="strided_attention",
     )(*inputs)
-    whole = jax.ShapeDtypeStruct((1, ROWS, 2 * WIDTH), BF16)
-    return pl.pallas_call(
+    outs = pl.pallas_call(
         hand_over,
-        out_shape=(whole, whole, whole, weight),
-        in_specs=[vmem] * 4,
-        out_specs=(vmem,) * 4,
+        out_shape=(tokens, tokens, tokens, weight),
+        in_specs=[hbm] * 4,
+        out_specs=(hbm,) * 4,
+        scratch_shapes=[pltpu.VMEM(a.shape, a.dtype) for a in outs] + [pltpu.SemaphoreType.DMA((2, 4))],
         name="hand_over",
     )(*outs)
+    return (outs[0][None], outs[1][None], outs[2][None], outs[3])
 
 
 def solution(mesh):

time: 124 us -> 101 us (0.81)
  Pallas kernels: 111 us -> 99.2 us
  local copies, waits for them, and re-layouts: 11.7 us -> 0 us
    unnamed x26 -> x0, local copies, waits for them, and re-layouts: 11.7 us -> none
    pallas_call x1, Pallas kernels: 109 us -> 97.1 us  [body(): pl.pallas_call(kernel, out_shape=(tokens, tokens, tokens, weight), in_spe...]
where the time goes in v3:
time: 101 us; the launch traced here: 99.8 us
  Pallas kernels  99.2 us (98%)
    pallas_call x1, Pallas kernels, body(): pl.pallas_call(kernel, out_shape=(tokens, tokens, tokens, weight), in_spe...  97.1 us
    pallas_call x1, Pallas kernels, body(): pl.pallas_call(hand_over, out_shape=(tokens, tokens, tokens, weight), in_...  2.07 us

profile of v3, /device:TPU:25, one launch (start us, length us, event | category | flops | bytes accessed | tf_op | source)
XLA Modules:
  0.0 99.8 jit_solution(1347672378988827459)
XLA Ops:
  0.6 97.1 %strided_attention.1 = (bf16[256,768]{1,0:T(8,128)(2,1)}, bf16[256,768]{1,0:T(8,128)(2,1)}, bf16[256,768]{1,0:T(8,128)(2,1)}, f32[6,768]{1,0:T(8,128)}) custom-call(bf16[256,768]{1,0:T(8,128)(2,1)} %bitcast.7, bf16[256,768]{1,0:T(8,128)(2,1)} %bitcast.8, bf16[256,768]{1,0:T(8,128)(2,1)} %bitcast.9, bf16[6,768]{1,0:T(8,128)(2,1)} %w_hbm.1, ...), custom_call_target="tpu_custom_call" | custom-call | flops 8000000000 | bytes 8000000 | tf_op jit(solution)/shard_map/strided_attention/pallas_call | solution.py:495
  97.7 2.1 %hand_over.1 = (bf16[256,768]{1,0:T(8,128)(2,1)}, bf16[256,768]{1,0:T(8,128)(2,1)}, bf16[256,768]{1,0:T(8,128)(2,1)}, f32[6,768]{1,0:T(8,128)}) custom-call(bf16[256,768]{1,0:T(8,128)(2,1)} %get-tuple-element.12.refs_0_, bf16[256,768]{1,0:T(8,128)(2,1)} %get-tuple-element.13.refs_1_, bf16[256,768]{1,0:T(8,128)(2,1)} %get-tuple-element.14.refs_2_, ...), custom_call_target="tpu_custom_call" | custom-call | tf_op jit(solution)/shard_map/hand_over/pallas_call | solution.py:553

commit v4 on v3

--- a/solution.py
+++ b/solution.py
@@ -47,8 +47,8 @@
     return [jnp.asarray(m, BF16) for m in (spread, gather, rows, pad, pad.T)]
 
 
-WZ, WX, WY, WC, RQ, RD, RT, G1, G2, G3, G4 = 8, 9, 10, 13, 17, 18, 19, 20, 22, 24, 25
-SEMS = 26
+WZ, WX, WC, RQ, RD, RT, G1, G2, G3, G4 = 8, 9, 10, 11, 12, 13, 14, 16, 18, 19
+SEMS = 20
 TILES = (4, 1, 1, 1, 1, 2, 1, 1)
 
 
@@ -61,7 +61,7 @@
     qc, kc, vc, dc, probs_ref, half_ref, ds_ref, att_a, dq_a, dk_a, dv_a,
     rs, rr, rs_do, rr_do, rt_s, rt_r, racc_k, racc_v, att_ref,
     g1_s, g1_r, g_own, g2_s, g2_r, g_sum, g3_s, g3_r, g4_s, g4_r,
-    isem, ssem, rsem,
+    isem, ssem, rsem, line_sem, plane_sem, core_sem,
 ):
     cs = (cs0, cs1, cs2, cs3, cs4, cs5, cs6, cs7)
     cr = (cr0, cr1, cr2, cr3, cr4, cr5, cr6, cr7)
@@ -119,23 +119,15 @@
 
     barrier = pltpu.get_barrier_semaphore()
 
-    def greet(where):
-        pl.semaphore_signal(barrier, inc=1, device_id=where, device_id_type=pl.DeviceIdType.MESH)
-
-    def greet_p(i, _):
-        greet(at_p(ring(p, i, GROUP)))
-        return 0
-
-    lax.fori_loop(1, GROUP, greet_p, 0)
-
-
-    def greet_chunk(i, _):
-        greet(at_chunk(ring(chunk, i, 16)))
-        return 0
-
-    lax.fori_loop(1, 16, greet_chunk, 0)
-    greet(at_core())
-    greet(((1 - yh) * 2 + 1 - core, ctx))
+    def greet(sem, where):
+        pl.semaphore_signal(sem, inc=1, device_id=where, device_id_type=pl.DeviceIdType.MESH)
+
+    for i in range(1, NZ):
+        greet(barrier, at_p(yl * 16 + ring(z, i, NZ)))
+    for i in range(1, 4):
+        greet(barrier, at_x(ring(x, i, 4)))
+        greet(barrier, at_y(ring(y, i, 4)))
+    greet(barrier, at_core())
     for load in loads[4:]:
         load.start()
 
@@ -153,14 +145,24 @@
         lax.fori_loop(0, 16, one, 0)
 
     def exchange(slot):
-        def one(i, _):
+        def own_line(i, _):
             half = lax.div(i + 1, 2)
             odd = lax.rem(i, 2)
-            pp = ring(p, odd * half + (1 - odd) * (GROUP - half), GROUP)
+            pp = yl * 16 + ring(z, odd * half + (1 - odd) * (NZ - half), NZ)
             send(cs[slot].at[pp], cr[slot].at[p], slot, at_p(pp))
             return 0
 
-        lax.fori_loop(1, GROUP, one, 0)
+        def other_line(i, _):
+            half = lax.div(i + 1, 2)
+            odd = lax.rem(i, 2)
+            pp = (1 - yl) * 16 + ring(z, odd * half + (1 - odd) * (NZ - half), NZ)
+            send(cs[slot].at[pp], cr[slot].at[p], slot, at_p(pp))
+            return 0
+
+        lax.fori_loop(1, NZ, own_line, 0)
+        if slot == 0:
+            pl.semaphore_wait(line_sem, 1)
+        lax.fori_loop(0, NZ, other_line, 0)
         cr[slot][p] = cs[slot][p]
 
     def unpack(slot, pairs):
@@ -196,7 +198,11 @@
             wz_rows[r * 3 + t : r * 3 + t + 1, :] = w[r : r + 1, t * 128 : (t + 1) * 128]
     wz_send[...] = wz_rows[...].astype(BF16)
     wz_recv[z] = wz_send[...]
-    pl.semaphore_wait(barrier, 48)
+    pl.semaphore_wait(barrier, 22)
+    greet(line_sem, at_p((1 - yl) * 16 + z))
+    for i in range(1, 4):
+        greet(plane_sem, at_x(ring(x, i, 4)))
+    greet(core_sem, at_core())
 
     def send_w(i, _):
         send(wz_send, wz_recv.at[z], WZ, at_p(yl * 16 + ring(z, i, NZ)))
@@ -217,32 +223,28 @@
 
     load_rows.wait()
     take(wz_recv.at[pl.ds(0, NZ - 1)], WZ)
-    at = yl * 4 + x
+    at = yh * 8 + yl * 4 + x
     gathered = wz_recv[...].reshape(256, 128)
     for t in range(3):
-        wg[core, yh, at, :, t * 128 : (t + 1) * 128] = dot(rows_ref[t], gathered).astype(BF16)
-    own = wg.at[core, yh, at]
-    for i in range(1, 4):
-        send(own, own, WX, at_x(ring(x, i, 4)))
+        wg[core, at, :, t * 128 : (t + 1) * 128] = dot(rows_ref[t], gathered).astype(BF16)
+    own = wg.at[core, at]
+    pl.semaphore_wait(plane_sem, 3)
+
+    def send_plane(i, _):
+        send(own, own, WX, at_chunk(ring(chunk, i, 16)))
+        return 0
+
+    lax.fori_loop(1, 16, send_plane, 0)
 
     load_c.wait()
     load_spread.wait()
     cot_p[...] = dot(c_ref[...], spread_ref[...]).astype(BF16)
 
-    mine = wg.at[core, yh, pl.ds(yl * 4, 4)]
-    take(wg.at[core, yh, pl.ds(0, 3)], WX)
-    for i in (1, 3, 2):
-        send(mine, mine, WY + i - 1, at_y(ring(y, i, 4)))
-    send(mine, mine, WC, at_core())
     load_gather.wait()
     cot_t[...] = dot(gather_ref[...], c_ref[...], NT).astype(BF16)
-    for i in (1, 3, 2):
-        yy = ring(y, 4 - i, 4)
-        part = wg.at[core, lax.div(yy, 2), pl.ds(lax.rem(yy, 2) * 4, 4)]
-        take(part, WY + i - 1)
-        send(part, part, WC + i, at_core())
-    for i in range(4):
-        take(mine, WC + i)
+    take(wg.at[core, pl.ds(0, 15)], WX)
+    send(wg.at[core], wg.at[core], WC, at_core())
+    take(wg.at[1 - core], WC)
 
     def grad_out(c):
         go[:, c * WIDTH : (c + 1) * WIDTH] = dot(
@@ -413,6 +415,7 @@
             for i in range(1, NZ):
                 total = total + g3_r[i].astype(F32)
             g4_s[...] = total
+            pl.semaphore_wait(core_sem, 1)
             for c in (1, 2, 3):
                 send(g4_s, g4_r, G4, (ring(dp, c, 4), ctx))
 
@@ -423,6 +426,7 @@
 
         @pl.when(jnp.logical_not(owner))
         def _():
+            pl.semaphore_wait(core_sem, 1)
             take(g4_r, G4)
 
         gw_ref[:, :WIDTH] = g4_r[0:6, :]
@@ -451,11 +455,8 @@
         sent(cs[slot].at[pl.ds(0, GROUP - 1)], slot)
     sent(wz_recv.at[pl.ds(0, NZ - 1)], WZ)
     sent(rs.at[pl.ds(0, 3)], RQ)
-    sent(wg.at[core, yh, pl.ds(0, 3)], WX)
-    for i in range(3):
-        sent(mine, WY + i)
-    for i in range(4):
-        sent(mine, WC + i)
+    sent(wg.at[core, pl.ds(0, 15)], WX)
+    sent(wg.at[core], WC)
     sent(rs_do.at[pl.ds(0, 3)], RD)
     sent(rt_s.at[pl.ds(0, 3)], RT)
     for g in range(2):
@@ -502,7 +503,7 @@
             pltpu.VMEM((16, 128), F32),
             pltpu.VMEM((16, 128), BF16),
             pltpu.VMEM((NZ, 16, 128), BF16),
-            pltpu.VMEM((2, 2, 8, 48, WIDTH), BF16),
+            pltpu.VMEM((2, 16, 48, WIDTH), BF16),
             pltpu.VMEM((ROWS, 768), BF16),
             pltpu.VMEM((1024, ROWS), BF16),
             pltpu.VMEM((ROWS, 2 * WIDTH), BF16),
@@ -541,6 +542,9 @@
             pltpu.SemaphoreType.DMA((len(inputs),)),
             pltpu.SemaphoreType.DMA((SEMS,)),
             pltpu.SemaphoreType.DMA((SEMS,)),
+            pltpu.SemaphoreType.REGULAR,
+            pltpu.SemaphoreType.REGULAR,
+            pltpu.SemaphoreType.REGULAR,
         ],
         compiler_params=pltpu.CompilerParams(
             collective_id=0, has_side_effects=True, vmem_limit_bytes=60 * 1024 * 1024

time: 101 us -> 102 us (level)
    pallas_call x1, Pallas kernels: 97.1 us -> 98.2 us  [body(): pl.pallas_call(kernel, out_shape=(tokens, tokens, tokens, weight), in_spe...]
where the time goes in v4:
time: 102 us; the launch traced here: 101 us
  Pallas kernels  100 us (98%)
    pallas_call x1, Pallas kernels, body(): pl.pallas_call(kernel, out_shape=(tokens, tokens, tokens, weight), in_spe...  98.2 us
    pallas_call x1, Pallas kernels, body(): pl.pallas_call(hand_over, out_shape=(tokens, tokens, tokens, weight), in_...  2.07 us

profile of v4, /device:TPU:25, one launch (start us, length us, event | category | flops | bytes accessed | tf_op | source)
XLA Modules:
  0.0 100.9 jit_solution(4019054344474572713)
XLA Ops:
  0.6 98.2 %strided_attention.1 = (bf16[256,768]{1,0:T(8,128)(2,1)}, bf16[256,768]{1,0:T(8,128)(2,1)}, bf16[256,768]{1,0:T(8,128)(2,1)}, f32[6,768]{1,0:T(8,128)}) custom-call(bf16[256,768]{1,0:T(8,128)(2,1)} %bitcast.7, bf16[256,768]{1,0:T(8,128)(2,1)} %bitcast.8, bf16[256,768]{1,0:T(8,128)(2,1)} %bitcast.9, bf16[6,768]{1,0:T(8,128)(2,1)} %w_hbm.1, ...), custom_call_target="tpu_custom_call" | custom-call | flops 8000000000 | bytes 8000000 | tf_op jit(solution)/shard_map/strided_attention/pallas_call | solution.py:496
  98.8 2.1 %hand_over.1 = (bf16[256,768]{1,0:T(8,128)(2,1)}, bf16[256,768]{1,0:T(8,128)(2,1)}, bf16[256,768]{1,0:T(8,128)(2,1)}, f32[6,768]{1,0:T(8,128)}) custom-call(bf16[256,768]{1,0:T(8,128)(2,1)} %get-tuple-element.12.refs_0_, bf16[256,768]{1,0:T(8,128)(2,1)} %get-tuple-element.13.refs_1_, bf16[256,768]{1,0:T(8,128)(2,1)} %get-tuple-element.14.refs_2_, ...), custom_call_target="tpu_custom_call" | custom-call | tf_op jit(solution)/shard_map/hand_over/pallas_call | solution.py:557

commit v5 on v3

--- a/solution.py
+++ b/solution.py
@@ -47,9 +47,10 @@
     return [jnp.asarray(m, BF16) for m in (spread, gather, rows, pad, pad.T)]
 
 
-WZ, WX, WY, WC, RQ, RD, RT, G1, G2, G3, G4 = 8, 9, 10, 13, 17, 18, 19, 20, 22, 24, 25
-SEMS = 26
-TILES = (4, 1, 1, 1, 1, 2, 1, 1)
+WZ, WX, WC, RQ, RD, RT, G1, G2, G3, G4 = 9, 10, 11, 12, 13, 14, 15, 17, 19, 20
+SEMS = 21
+TILES = (4, 1, 1, 1, 1, 1, 1, 1, 1)
+LAST_ORDER = (0, 1, 2, 3, 4, 15, 5, 14, 6, 13, 7, 12, 8, 9, 10, 11)
 
 
 def kernel(
@@ -57,14 +58,14 @@
     gq_ref, gk_ref, gv_ref, gw_ref,
     q_ref, k_ref, v_ref, w_ref, c_ref, spread_ref, gather_ref, rows_ref, pad_ref, unpad_ref,
     wz_rows, wz_send, wz_recv, wg, cot_p, cot_t, go,
-    cs0, cs1, cs2, cs3, cs4, cs5, cs6, cs7, cr0, cr1, cr2, cr3, cr4, cr5, cr6, cr7,
+    cs0, cs1, cs2, cs3, cs4, cs5, cs6, cs7, cs8, cr0, cr1, cr2, cr3, cr4, cr5, cr6, cr7, cr8,
     qc, kc, vc, dc, probs_ref, half_ref, ds_ref, att_a, dq_a, dk_a, dv_a,
     rs, rr, rs_do, rr_do, rt_s, rt_r, racc_k, racc_v, att_ref,
     g1_s, g1_r, g_own, g2_s, g2_r, g_sum, g3_s, g3_r, g4_s, g4_r,
     isem, ssem, rsem,
 ):
-    cs = (cs0, cs1, cs2, cs3, cs4, cs5, cs6, cs7)
-    cr = (cr0, cr1, cr2, cr3, cr4, cr5, cr6, cr7)
+    cs = (cs0, cs1, cs2, cs3, cs4, cs5, cs6, cs7, cs8)
+    cr = (cr0, cr1, cr2, cr3, cr4, cr5, cr6, cr7, cr8)
     dp, ctx = lax.axis_index("dp"), lax.axis_index("ctx")
     core, yh = lax.rem(dp, 2), lax.div(dp, 2)
     x, p = lax.rem(ctx, 4), lax.div(ctx, 4)
@@ -160,7 +161,17 @@
             send(cs[slot].at[pp], cr[slot].at[p], slot, at_p(pp))
             return 0
 
-        lax.fori_loop(1, GROUP, one, 0)
+        if slot < len(TILES) - 1:
+            lax.fori_loop(1, GROUP, one, 0)
+        else:
+            for zz in LAST_ORDER:
+                for by in range(2):
+                    pp = ring(yl, by, 2) * 16 + zz
+
+                    @pl.when(pp != p)
+                    def _():
+                        send(cs[slot].at[pp], cr[slot].at[p], slot, at_p(pp))
+
         cr[slot][p] = cs[slot][p]
 
     def unpack(slot, pairs):
@@ -217,32 +228,27 @@
 
     load_rows.wait()
     take(wz_recv.at[pl.ds(0, NZ - 1)], WZ)
-    at = yl * 4 + x
+    at = yh * 8 + yl * 4 + x
     gathered = wz_recv[...].reshape(256, 128)
     for t in range(3):
-        wg[core, yh, at, :, t * 128 : (t + 1) * 128] = dot(rows_ref[t], gathered).astype(BF16)
-    own = wg.at[core, yh, at]
-    for i in range(1, 4):
-        send(own, own, WX, at_x(ring(x, i, 4)))
+        wg[core, at, :, t * 128 : (t + 1) * 128] = dot(rows_ref[t], gathered).astype(BF16)
+    own = wg.at[core, at]
+
+    def send_plane(i, _):
+        send(own, own, WX, at_chunk(ring(chunk, i, 16)))
+        return 0
+
+    lax.fori_loop(1, 16, send_plane, 0)
 
     load_c.wait()
     load_spread.wait()
     cot_p[...] = dot(c_ref[...], spread_ref[...]).astype(BF16)
 
-    mine = wg.at[core, yh, pl.ds(yl * 4, 4)]
-    take(wg.at[core, yh, pl.ds(0, 3)], WX)
-    for i in (1, 3, 2):
-        send(mine, mine, WY + i - 1, at_y(ring(y, i, 4)))
-    send(mine, mine, WC, at_core())
     load_gather.wait()
     cot_t[...] = dot(gather_ref[...], c_ref[...], NT).astype(BF16)
-    for i in (1, 3, 2):
-        yy = ring(y, 4 - i, 4)
-        part = wg.at[core, lax.div(yy, 2), pl.ds(lax.rem(yy, 2) * 4, 4)]
-        take(part, WY + i - 1)
-        send(part, part, WC + i, at_core())
-    for i in range(4):
-        take(mine, WC + i)
+    take(wg.at[core, pl.ds(0, 15)], WX)
+    send(wg.at[core], wg.at[core], WC, at_core())
+    take(wg.at[1 - core], WC)
 
     def grad_out(c):
         go[:, c * WIDTH : (c + 1) * WIDTH] = dot(
@@ -355,15 +361,14 @@
         attend(h)
     pack(4, [((att_a, 128), (att_a, 256))])
     exchange(4)
+    pack(5, [((dk_a, 0), (dv_a, 0))])
+    exchange(5)
     for h in (2, 3):
         score_grads(h)
-    pack(5, [((dk_a, 0), (dv_a, 0)), ((dq_a, 128), (dq_a, 256))])
-    exchange(5)
-    for h in (2, 3):
         key_grads(h)
-    pack(6, [((dk_a, 128), (dk_a, 256))])
-    exchange(6)
-    pack(7, [((dv_a, 128), (dv_a, 256))])
+    pack(6, [((dq_a, 128), (dq_a, 256))])
+    pack(7, [((dk_a, 128), (dk_a, 256))])
+    pack(8, [((dv_a, 128), (dv_a, 256))])
 
     def reduce_core(g):
         attended = att_ref[:, g * WIDTH : (g + 1) * WIDTH]
@@ -434,28 +439,28 @@
         heads = jnp.concatenate([rt_r[h, index] for h in range(HEADS)], axis=1)
         ref[:, :WIDTH] = dot(heads, unpad_ref[...]).astype(BF16)
     reduce_core(0)
+    reduce_plane(0)
     unpack(3, [((att_ref, WIDTH), (gq_ref, WIDTH))])
     unpack(4, [((att_ref, WIDTH + 128), (att_ref, WIDTH + 256))])
     reduce_core(1)
-    reduce_plane(0)
+    exchange(6)
+    exchange(7)
     reduce_plane(1)
     reduce_z()
-    exchange(7)
-    unpack(5, [((gk_ref, WIDTH), (gv_ref, WIDTH)), ((gq_ref, WIDTH + 128), (gq_ref, WIDTH + 256))])
+    exchange(8)
+    unpack(5, [((gk_ref, WIDTH), (gv_ref, WIDTH))])
+    unpack(6, [((gq_ref, WIDTH + 128), (gq_ref, WIDTH + 256))])
+    unpack(7, [((gk_ref, WIDTH + 128), (gk_ref, WIDTH + 256))])
     reduce_last()
-    unpack(6, [((gk_ref, WIDTH + 128), (gk_ref, WIDTH + 256))])
+    unpack(8, [((gv_ref, WIDTH + 128), (gv_ref, WIDTH + 256))])
     finish()
-    unpack(7, [((gv_ref, WIDTH + 128), (gv_ref, WIDTH + 256))])
-
-    for slot in range(8):
+
+    for slot in range(9):
         sent(cs[slot].at[pl.ds(0, GROUP - 1)], slot)
     sent(wz_recv.at[pl.ds(0, NZ - 1)], WZ)
     sent(rs.at[pl.ds(0, 3)], RQ)
-    sent(wg.at[core, yh, pl.ds(0, 3)], WX)
-    for i in range(3):
-        sent(mine, WY + i)
-    for i in range(4):
-        sent(mine, WC + i)
+    sent(wg.at[core, pl.ds(0, 15)], WX)
+    sent(wg.at[core], WC)
     sent(rs_do.at[pl.ds(0, 3)], RD)
     sent(rt_s.at[pl.ds(0, 3)], RT)
     for g in range(2):
@@ -502,7 +507,7 @@
             pltpu.VMEM((16, 128), F32),
             pltpu.VMEM((16, 128), BF16),
             pltpu.VMEM((NZ, 16, 128), BF16),
-            pltpu.VMEM((2, 2, 8, 48, WIDTH), BF16),
+            pltpu.VMEM((2, 16, 48, WIDTH), BF16),
             pltpu.VMEM((ROWS, 768), BF16),
             pltpu.VMEM((1024, ROWS), BF16),
             pltpu.VMEM((ROWS, 2 * WIDTH), BF16),

time: 101 us -> 97.6 us (0.966)
  Pallas kernels: 99.2 us -> 96.2 us
    pallas_call x1, Pallas kernels: 97.1 us -> 94.1 us  [body(): pl.pallas_call(kernel, out_shape=(tokens, tokens, tokens, weight), in_spe...]
where the time goes in v5:
time: 97.6 us; the launch traced here: 96.8 us
  Pallas kernels  96.2 us (99%)
    pallas_call x1, Pallas kernels, body(): pl.pallas_call(kernel, out_shape=(tokens, tokens, tokens, weight), in_spe...  94.1 us
    pallas_call x1, Pallas kernels, body(): pl.pallas_call(hand_over, out_shape=(tokens, tokens, tokens, weight), in_...  2.07 us

profile of v5, /device:TPU:25, one launch (start us, length us, event | category | flops | bytes accessed | tf_op | source)
XLA Modules:
  0.0 96.8 jit_solution(3109269825664523186)
XLA Ops:
  0.6 94.1 %strided_attention.1 = (bf16[256,768]{1,0:T(8,128)(2,1)}, bf16[256,768]{1,0:T(8,128)(2,1)}, bf16[256,768]{1,0:T(8,128)(2,1)}, f32[6,768]{1,0:T(8,128)}) custom-call(bf16[256,768]{1,0:T(8,128)(2,1)} %bitcast.7, bf16[256,768]{1,0:T(8,128)(2,1)} %bitcast.8, bf16[256,768]{1,0:T(8,128)(2,1)} %bitcast.9, bf16[6,768]{1,0:T(8,128)(2,1)} %w_hbm.1, ...), custom_call_target="tpu_custom_call" | custom-call | flops 8000000000 | bytes 8000000 | tf_op jit(solution)/shard_map/strided_attention/pallas_call | solution.py:500
  94.7 2.1 %hand_over.1 = (bf16[256,768]{1,0:T(8,128)(2,1)}, bf16[256,768]{1,0:T(8,128)(2,1)}, bf16[256,768]{1,0:T(8,128)(2,1)}, f32[6,768]{1,0:T(8,128)}) custom-call(bf16[256,768]{1,0:T(8,128)(2,1)} %get-tuple-element.12.refs_0_, bf16[256,768]{1,0:T(8,128)(2,1)} %get-tuple-element.13.refs_1_, bf16[256,768]{1,0:T(8,128)(2,1)} %get-tuple-element.14.refs_2_, ...), custom_call_target="tpu_custom_call" | custom-call | tf_op jit(solution)/shard_map/hand_over/pallas_call | solution.py:558

commit v6 on v5

--- a/solution.py
+++ b/solution.py
@@ -55,14 +55,14 @@
 
 def kernel(
     q_hbm, k_hbm, v_hbm, w_hbm, c_hbm, spread_hbm, gather_hbm, rows_hbm, pad_hbm, unpad_hbm,
-    gq_ref, gk_ref, gv_ref, gw_ref,
+    gq_hbm, gk_hbm, gv_hbm, gw_hbm,
     q_ref, k_ref, v_ref, w_ref, c_ref, spread_ref, gather_ref, rows_ref, pad_ref, unpad_ref,
     wz_rows, wz_send, wz_recv, wg, cot_p, cot_t, go,
     cs0, cs1, cs2, cs3, cs4, cs5, cs6, cs7, cs8, cr0, cr1, cr2, cr3, cr4, cr5, cr6, cr7, cr8,
     qc, kc, vc, dc, probs_ref, half_ref, ds_ref, att_a, dq_a, dk_a, dv_a,
     rs, rr, rs_do, rr_do, rt_s, rt_r, racc_k, racc_v, att_ref,
     g1_s, g1_r, g_own, g2_s, g2_r, g_sum, g3_s, g3_r, g4_s, g4_r,
-    isem, ssem, rsem,
+    gq_ref, gk_ref, gv_ref, gw_ref, osem, isem, ssem, rsem,
 ):
     cs = (cs0, cs1, cs2, cs3, cs4, cs5, cs6, cs7, cs8)
     cr = (cr0, cr1, cr2, cr3, cr4, cr5, cr6, cr7, cr8)
@@ -87,6 +87,13 @@
      load_unpad) = loads
     for load in loads[:4]:
         load.start()
+
+    stores = [
+        pltpu.make_async_copy(src, dst, osem.at[i])
+        for i, (src, dst) in enumerate(
+            ((gq_ref, gq_hbm), (gk_ref, gk_hbm), (gv_ref, gv_hbm), (gw_ref, gw_hbm))
+        )
+    ]
 
     def at_p(pp):
         return (dp, pp * 4 + x)
@@ -450,10 +457,14 @@
     exchange(8)
     unpack(5, [((gk_ref, WIDTH), (gv_ref, WIDTH))])
     unpack(6, [((gq_ref, WIDTH + 128), (gq_ref, WIDTH + 256))])
+    stores[0].start()
     unpack(7, [((gk_ref, WIDTH + 128), (gk_ref, WIDTH + 256))])
+    stores[1].start()
     reduce_last()
     unpack(8, [((gv_ref, WIDTH + 128), (gv_ref, WIDTH + 256))])
+    stores[2].start()
     finish()
+    stores[3].start()
 
     for slot in range(9):
         sent(cs[slot].at[pl.ds(0, GROUP - 1)], slot)
@@ -475,13 +486,21 @@
     @pl.when(jnp.logical_not(owner))
     def _():
         sent(g3_s, G3)
+    for store in stores:
+        store.wait()
 
 
 def hand_over(*refs):
     n = 4
     srcs, dsts, held, sems = refs[:n], refs[n : 2 * n], refs[2 * n : 3 * n], refs[3 * n]
-    inward = [pltpu.make_async_copy(a, b, sems.at[0, i]) for i, (a, b) in enumerate(zip(srcs, held, strict=True))]
-    outward = [pltpu.make_async_copy(a, b, sems.at[1, i]) for i, (a, b) in enumerate(zip(held, dsts, strict=True))]
+    inward, outward = [], []
+    for src, dst, mid in zip(srcs, dsts, held, strict=True):
+        half = ROWS // 2
+        pieces = (pl.ds(0, half), pl.ds(half, half)) if src.shape[0] == ROWS else (pl.ds(0, src.shape[0]),)
+        for piece in pieces:
+            i = len(inward)
+            inward.append(pltpu.make_async_copy(src.at[piece], mid.at[piece], sems.at[0, i]))
+            outward.append(pltpu.make_async_copy(mid.at[piece], dst.at[piece], sems.at[1, i]))
     for copy in inward:
         copy.start()
     for first, second in zip(inward, outward, strict=True):
@@ -492,7 +511,7 @@
 
 
 def body(queries, key_rows, value_rows, out_weight, cotangent, *matrices):
-    vmem, hbm = pl.BlockSpec(memory_space=pltpu.VMEM), pl.BlockSpec(memory_space=pltpu.HBM)
+    hbm = pl.BlockSpec(memory_space=pltpu.HBM)
     tokens = jax.ShapeDtypeStruct((ROWS, 2 * WIDTH), BF16)
     weight = jax.ShapeDtypeStruct((6, 2 * WIDTH), F32)
     inputs = (queries[0], key_rows[0], value_rows[0], out_weight, cotangent[0], *matrices)
@@ -501,7 +520,7 @@
         kernel,
         out_shape=(tokens, tokens, tokens, weight),
         in_specs=[hbm] * len(inputs),
-        out_specs=(vmem,) * 4,
+        out_specs=(hbm,) * 4,
         scratch_shapes=[pltpu.VMEM(a.shape, a.dtype) for a in inputs]
         + [
             pltpu.VMEM((16, 128), F32),
@@ -543,6 +562,11 @@
             pltpu.VMEM((NZ, 16, WIDTH), BF16),
             pltpu.VMEM((16, WIDTH), F32),
             pltpu.VMEM((16, WIDTH), F32),
+            pltpu.VMEM(tokens.shape, BF16),
+            pltpu.VMEM(tokens.shape, BF16),
+            pltpu.VMEM(tokens.shape, BF16),
+            pltpu.VMEM(weight.shape, F32),
+            pltpu.SemaphoreType.DMA((4,)),
             pltpu.SemaphoreType.DMA((len(inputs),)),
             pltpu.SemaphoreType.DMA((SEMS,)),
             pltpu.SemaphoreType.DMA((SEMS,)),
@@ -560,7 +584,7 @@
         out_shape=(tokens, tokens, tokens, weight),
         in_specs=[hbm] * 4,
         out_specs=(hbm,) * 4,
-        scratch_shapes=[pltpu.VMEM(a.shape, a.dtype) for a in outs] + [pltpu.SemaphoreType.DMA((2, 4))],
+        scratch_shapes=[pltpu.VMEM(a.shape, a.dtype) for a in outs] + [pltpu.SemaphoreType.DMA((2, 7))],
         name="hand_over",
     )(*outs)
     return (outs[0][None], outs[1][None], outs[2][None], outs[3])

time: 97.6 us -> 97.3 us (level)
  no operation moved by 1% of the time
where the time goes in v6:
time: 97.3 us; the launch traced here: 97.1 us
  Pallas kernels  96.5 us (99%)
    pallas_call x1, Pallas kernels, body(): pl.pallas_call(kernel, out_shape=(tokens, tokens, tokens, weight), in_spe...  94.3 us
    pallas_call x1, Pallas kernels, body(): pl.pallas_call(hand_over, out_shape=(tokens, tokens, tokens, weight), in_...  2.15 us

profile of v6, /device:TPU:25, one launch (start us, length us, event | category | flops | bytes accessed | tf_op | source)
XLA Modules:
  0.0 97.1 jit_solution(18375578774196534984)
XLA Ops:
  0.6 94.3 %strided_attention.1 = (bf16[256,768]{1,0:T(8,128)(2,1)}, bf16[256,768]{1,0:T(8,128)(2,1)}, bf16[256,768]{1,0:T(8,128)(2,1)}, f32[6,768]{1,0:T(8,128)}) custom-call(bf16[256,768]{1,0:T(8,128)(2,1)} %bitcast.7, bf16[256,768]{1,0:T(8,128)(2,1)} %bitcast.8, bf16[256,768]{1,0:T(8,128)(2,1)} %bitcast.9, bf16[6,768]{1,0:T(8,128)(2,1)} %w_hbm.1, ...), custom_call_target="tpu_custom_call" | custom-call | flops 8000000000 | bytes 8000000 | tf_op jit(solution)/shard_map/strided_attention/pallas_call | solution.py:519
  94.9 2.1 %hand_over.1 = (bf16[256,768]{1,0:T(8,128)(2,1)}, bf16[256,768]{1,0:T(8,128)(2,1)}, bf16[256,768]{1,0:T(8,128)(2,1)}, f32[6,768]{1,0:T(8,128)}) custom-call(bf16[256,768]{1,0:T(8,128)(2,1)} %get-tuple-element.12.refs_0_, bf16[256,768]{1,0:T(8,128)(2,1)} %get-tuple-element.13.refs_1_, bf16[256,768]{1,0:T(8,128)(2,1)} %get-tuple-element.14.refs_2_, ...), custom_call_target="tpu_custom_call" | custom-call | tf_op jit(solution)/shard_map/hand_over/pallas_call | solution.py:582

commit v7 on v6

--- a/solution.py
+++ b/solution.py
@@ -50,7 +50,7 @@
 WZ, WX, WC, RQ, RD, RT, G1, G2, G3, G4 = 9, 10, 11, 12, 13, 14, 15, 17, 19, 20
 SEMS = 21
 TILES = (4, 1, 1, 1, 1, 1, 1, 1, 1)
-LAST_ORDER = (0, 1, 2, 3, 4, 15, 5, 14, 6, 13, 7, 12, 8, 9, 10, 11)
+EARLY_PLANES, LATE_PLANES = (0, 1, 2, 3), (4, 15, 5, 14, 6, 13, 7, 12, 8, 9, 10, 11)
 
 
 def kernel(
@@ -160,7 +160,7 @@
 
         lax.fori_loop(0, 16, one, 0)
 
-    def exchange(slot):
+    def exchange(slot, planes=None):
         def one(i, _):
             half = lax.div(i + 1, 2)
             odd = lax.rem(i, 2)
@@ -168,10 +168,10 @@
             send(cs[slot].at[pp], cr[slot].at[p], slot, at_p(pp))
             return 0
 
-        if slot < len(TILES) - 1:
+        if planes is None:
             lax.fori_loop(1, GROUP, one, 0)
         else:
-            for zz in LAST_ORDER:
+            for zz in planes:
                 for by in range(2):
                     pp = ring(yl, by, 2) * 16 + zz
 
@@ -179,7 +179,8 @@
                     def _():
                         send(cs[slot].at[pp], cr[slot].at[p], slot, at_p(pp))
 
-        cr[slot][p] = cs[slot][p]
+        if planes is not LATE_PLANES:
+            cr[slot][p] = cs[slot][p]
 
     def unpack(slot, pairs):
         take(cr[slot].at[pl.ds(0, GROUP - 1)], slot)
@@ -450,11 +451,13 @@
     unpack(3, [((att_ref, WIDTH), (gq_ref, WIDTH))])
     unpack(4, [((att_ref, WIDTH + 128), (att_ref, WIDTH + 256))])
     reduce_core(1)
-    exchange(6)
-    exchange(7)
+    for slot in (6, 7, 8):
+        exchange(slot, EARLY_PLANES)
+    for slot in (6, 7):
+        exchange(slot, LATE_PLANES)
     reduce_plane(1)
     reduce_z()
-    exchange(8)
+    exchange(8, LATE_PLANES)
     unpack(5, [((gk_ref, WIDTH), (gv_ref, WIDTH))])
     unpack(6, [((gq_ref, WIDTH + 128), (gq_ref, WIDTH + 256))])
     stores[0].start()

time: 97.3 us -> 97.4 us (level)
  no operation moved by 1% of the time
where the time goes in v7:
time: 97.4 us; the launch traced here: 97.2 us
  Pallas kernels  96.6 us (99%)
    pallas_call x1, Pallas kernels, body(): pl.pallas_call(kernel, out_shape=(tokens, tokens, tokens, weight), in_spe...  94.4 us
    pallas_call x1, Pallas kernels, body(): pl.pallas_call(hand_over, out_shape=(tokens, tokens, tokens, weight), in_...  2.15 us

profile of v7, /device:TPU:25, one launch (start us, length us, event | category | flops | bytes accessed | tf_op | source)
XLA Modules:
  0.0 97.2 jit_solution(3791551194850726562)
XLA Ops:
  0.6 94.4 %strided_attention.1 = (bf16[256,768]{1,0:T(8,128)(2,1)}, bf16[256,768]{1,0:T(8,128)(2,1)}, bf16[256,768]{1,0:T(8,128)(2,1)}, f32[6,768]{1,0:T(8,128)}) custom-call(bf16[256,768]{1,0:T(8,128)(2,1)} %bitcast.7, bf16[256,768]{1,0:T(8,128)(2,1)} %bitcast.8, bf16[256,768]{1,0:T(8,128)(2,1)} %bitcast.9, bf16[6,768]{1,0:T(8,128)(2,1)} %w_hbm.1, ...), custom_call_target="tpu_custom_call" | custom-call | flops 8000000000 | bytes 8000000 | tf_op jit(solution)/shard_map/strided_attention/pallas_call | solution.py:522
  95.1 2.1 %hand_over.1 = (bf16[256,768]{1,0:T(8,128)(2,1)}, bf16[256,768]{1,0:T(8,128)(2,1)}, bf16[256,768]{1,0:T(8,128)(2,1)}, f32[6,768]{1,0:T(8,128)}) custom-call(bf16[256,768]{1,0:T(8,128)(2,1)} %get-tuple-element.12.refs_0_, bf16[256,768]{1,0:T(8,128)(2,1)} %get-tuple-element.13.refs_1_, bf16[256,768]{1,0:T(8,128)(2,1)} %get-tuple-element.14.refs_2_, ...), custom_call_target="tpu_custom_call" | custom-call | tf_op jit(solution)/shard_map/hand_over/pallas_call | solution.py:585
